TPU v7x, 256 devices: a whole 4x4x8 slice. The times are simulated.
256 devices in a mesh: ctx: 32 (over y, x, core), head: 8 (over z).
Axes of the slice: x: 4, y: 4, z: 8, core: 2. Of those that a mesh axis runs over, the one named last changes fastest.
Arguments:
- latents: bfloat16 [131072, 576], P('ctx'), may hold values from -8 to 8
- idx_keys: bfloat16 [131072, 128], P('ctx'), may hold values from -8 to 8
- mla_query: bfloat16 [4096, 128, 576], P('ctx', 'head'), may hold values from -32 to 32
- idx_query: bfloat16 [4096, 64, 128], P('ctx', 'head'), may hold values from -100 to 100
- idx_weight: bfloat16 [4096, 64], P('ctx', 'head'), may hold values from -1.5 to 1.5
- sel_blocks: int32 [64, 32], P('ctx'), may hold values from 0 to 2047, as said below
Outputs:
- kl: float32 [4096], P(('ctx', 'head'))
- grad_query: float32 [4096, 64, 128], P('ctx', 'head')
- grad_weight: float32 [4096, 64], P('ctx', 'head')
- grad_keys: float32 [2048, 64, 128], P('ctx', 'head')
Inputs may be any that keep to these rules, and one draw needn't show every extreme that they name: `sel_blocks`: row r lists 32 different key blocks, none after block 1984 + r. At most 2 of a row's blocks lie in the range of 4096 keys of one index of ctx, and in every draw one such range holds exactly 2 blocks of every row.
All inputs are finite; a program needn't handle non-finite values.
Results may differ from a plain program's by a relative error of at most 0.018.
Values may be sent and summed in bfloat16 or wider, within the bound.
A program may use at most 128 MiB of HBM per device.

v0:
```python
import jax
import jax.numpy as jnp
from jax import lax
from jax.sharding import PartitionSpec as P

LAT = 576
DI = 128
BLK = 64


MLA_SCALE = 192.0 ** (-0.5)
FLOOR_SCORE = -1e30


def finish(target, logits, visible, span_keys):
    masked = jnp.where(visible, logits, FLOOR_SCORE)
    shifted = masked - jnp.max(masked, axis=-1, keepdims=True)
    log_norm = jnp.log(jnp.sum(jnp.exp(shifted), axis=-1, keepdims=True))
    log_ratio = shifted - log_norm
    predicted = jnp.where(visible, jnp.exp(log_ratio), 0.0)
    positive = target > 0.0
    entropy = jnp.sum(
        jnp.where(positive, target * jnp.log(jnp.where(positive, target, 1.0)), 0.0), axis=-1
    )
    cross_term = jnp.sum(jnp.where(visible, target * log_ratio, 0.0), axis=-1)
    divergence = entropy - cross_term
    gradient = jnp.where(visible, span_keys * (predicted - target), 0.0).astype(jnp.bfloat16)
    return (divergence, gradient)


def local(latents, idx_keys, mla_query, idx_query, idx_weight, sel_blocks):
    ctx_count = lax.axis_size("ctx")
    head_count = lax.axis_size("head")
    ctx_index = lax.axis_index("ctx")
    head_index = lax.axis_index("head")
    key_local = latents.shape[0]
    local_blocks = key_local // BLK
    query_local = mla_query.shape[0]
    heads_local = mla_query.shape[1]
    index_heads = idx_query.shape[1]
    block_rows, chosen_count = sel_blocks.shape
    capacity = max(2, 2 * chosen_count // ctx_count)
    slot_count = block_rows * capacity
    span_keys = chosen_count * BLK
    all_heads = heads_local * head_count
    context_len = key_local * ctx_count
    window_len = query_local * ctx_count
    rows_share = query_local // head_count
    index_scale = DI ** (-0.5)
    owners = sel_blocks // local_blocks
    inside = sel_blocks - owners * local_blocks
    positions = jnp.arange(chosen_count, dtype=jnp.int32)
    same_owner = owners[:, :, None] == owners[:, None, :]
    earlier = positions[None, :] < positions[:, None]
    ranks = jnp.sum((same_owner & earlier[None, :, :]).astype(jnp.int32), axis=2)
    in_row = owners * capacity + ranks
    slot_ids = jnp.arange(ctx_count * capacity, dtype=jnp.int32)
    matches = in_row[:, :, None] == slot_ids[None, None, :]
    request_table = jnp.sum(jnp.where(matches, inside[:, :, None] + 1, 0), axis=1) - 1
    requests = (
        request_table.reshape(block_rows, ctx_count, capacity)
        .transpose(1, 0, 2)
        .reshape(ctx_count, slot_count)
    )
    wanted = lax.all_to_all(requests, "ctx", split_axis=0, concat_axis=0, tiled=True)
    present = wanted >= 0
    safe_ids = jnp.maximum(wanted, 0)
    lat_table = latents.reshape(local_blocks, BLK * LAT)
    key_table = idx_keys.reshape(local_blocks, BLK * DI)
    empty_value = jnp.zeros((), jnp.bfloat16)
    lat_out = jnp.where(present[:, :, None], jnp.take(lat_table, safe_ids, axis=0), empty_value)
    key_out = jnp.where(present[:, :, None], jnp.take(key_table, safe_ids, axis=0), empty_value)
    lat_back, key_back = (
        lax.all_to_all(lat_out, "ctx", split_axis=0, concat_axis=0, tiled=True),
        lax.all_to_all(key_out, "ctx", split_axis=0, concat_axis=0, tiled=True),
    )
    row_base = jnp.arange(block_rows, dtype=jnp.int32)[:, None] * capacity
    flat_slot = (owners * slot_count + row_base + ranks).reshape(-1)
    lat_dense = jnp.take(
        lat_back.reshape(ctx_count * slot_count, BLK * LAT), flat_slot, axis=0
    ).reshape(block_rows, span_keys, LAT)
    key_dense = jnp.take(
        key_back.reshape(ctx_count * slot_count, BLK * DI), flat_slot, axis=0
    ).reshape(block_rows, span_keys, DI)
    offsets = jnp.arange(BLK, dtype=jnp.int32)
    key_pos = (sel_blocks[:, :, None] * BLK + offsets[None, None, :]).reshape(block_rows, span_keys)
    query_pos = (
        context_len
        - window_len
        + ctx_index * query_local
        + jnp.arange(query_local, dtype=jnp.int32).reshape(block_rows, BLK)
    )
    visible = key_pos[:, None, :] <= query_pos[:, :, None]
    query_blocks = mla_query.reshape(block_rows, BLK, heads_local, LAT)
    index_blocks = idx_query.reshape(block_rows, BLK, index_heads, DI)
    weight_blocks = idx_weight.reshape(block_rows, BLK, index_heads)

    def forward_block(pieces):
        queries, lat_rows, key_rows, index_query, weights, seen = pieces
        raw_scores = jnp.einsum(
            "qhl,kl->qhk", queries, lat_rows, preferred_element_type=jnp.float32
        )
        seen_heads = seen[:, None, :]
        peak = jnp.max(jnp.where(seen_heads, raw_scores, FLOOR_SCORE), axis=-1, keepdims=True)
        total = jnp.sum(
            jnp.where(seen_heads, jnp.exp(MLA_SCALE * (raw_scores - peak)), 0.0),
            axis=-1,
            keepdims=True,
        )
        inverse = 1.0 / (total * all_heads)
        target_part = jnp.sum(
            jnp.where(seen_heads, jnp.exp(MLA_SCALE * (raw_scores - peak)) * inverse, 0.0), axis=1
        )
        dots = jnp.einsum("qjd,kd->qjk", index_query, key_rows, preferred_element_type=jnp.float32)
        logit_part = jnp.sum(
            (weights.astype(jnp.float32) * index_scale)[:, :, None] * jnp.maximum(dots, 0.0), axis=1
        )
        return (target_part, logit_part)

    target_part, logit_part = lax.map(
        forward_block, (query_blocks, lat_dense, key_dense, index_blocks, weight_blocks, visible)
    )
    target, logits = lax.psum((target_part, logit_part), "head")
    divergence, gradient = finish(target, logits, visible, span_keys)
    kl_rows = lax.dynamic_slice_in_dim(
        divergence.reshape(query_local), head_index * rows_share, rows_share, 0
    )

    def backward_block(pieces):
        key_rows, index_query, weights, grad_block = pieces
        dots = (
            jnp.einsum("qjd,kd->qjk", index_query, key_rows, preferred_element_type=jnp.float32)
            * index_scale
        )
        grad_f = grad_block.astype(jnp.float32)
        weight_grad = jnp.sum(grad_f[:, None, :] * jnp.maximum(dots, 0.0), axis=2)
        factor = (
            grad_f[:, None, :]
            * weights.astype(jnp.float32)[:, :, None]
            * jnp.where(dots > 0.0, index_scale, 0.0)
        ).astype(jnp.bfloat16)
        query_grad = jnp.einsum("qjk,kd->qjd", factor, key_rows, preferred_element_type=jnp.float32)
        key_grad = jnp.einsum(
            "qjk,qjd->kd", factor, index_query, preferred_element_type=jnp.float32
        )
        return (weight_grad, query_grad, key_grad)

    weight_grad, query_grad, key_grad = lax.map(
        backward_block, (key_dense, index_blocks, weight_blocks, gradient)
    )
    slot_grads = jnp.zeros((ctx_count * slot_count, BLK * DI), jnp.float32)
    slot_grads = slot_grads.at[flat_slot].set(key_grad.reshape(block_rows * chosen_count, BLK * DI))
    slot_grads = slot_grads.reshape(ctx_count, slot_count, BLK, DI)
    arrived = lax.all_to_all(
        slot_grads.astype(jnp.bfloat16), "ctx", split_axis=0, concat_axis=0, tiled=True
    ).astype(slot_grads.dtype)
    rows_each = arrived.shape[2]
    block_ids = jnp.arange(local_blocks, dtype=jnp.int32)
    one_hot = (wanted.reshape(-1)[None, :] == block_ids[:, None]).astype(jnp.float32)
    summed = jnp.dot(
        one_hot,
        arrived.reshape(ctx_count * slot_count, rows_each * DI),
        precision=lax.Precision.HIGHEST,
    ).reshape(local_blocks, rows_each, DI)
    key_result = lax.psum_scatter(
        summed.astype(jnp.bfloat16), "head", scatter_dimension=1, tiled=True
    ).astype(jnp.float32)
    grad_query = query_grad.reshape(query_local, index_heads, DI)
    grad_weight = weight_grad.reshape(query_local, index_heads)
    return (kl_rows, grad_query, grad_weight, key_result)


def solution(mesh):
    in_specs = (
        P("ctx", None),
        P("ctx", None),
        P("ctx", "head", None),
        P("ctx", "head", None),
        P("ctx", "head"),
        P("ctx", None),
    )
    out_specs = (
        P(("ctx", "head")),
        P("ctx", "head", None),
        P("ctx", "head"),
        P("ctx", "head", None),
    )
    return jax.shard_map(local, mesh=mesh, in_specs=in_specs, out_specs=out_specs, check_vma=False)
```

profile of v0, /device:TPU:2, one launch (start us, length us, event | category | flops | bytes accessed | tf_op | source)
XLA Modules:
  0.0 514.5 jit_solution(11037304357760015870)
XLA Ops:
  7.2 0.7 subtract_add_fusion
  8.4 0.7 copy.73
  9.1 7.6 %all-to-all-start = ((s32[32,1,4]{2,1,0:T(1,128)}), s32[32,1,4]{2,1,0:T(1,128)S(1)}, u32[]{:S(2)}, u32[]{:S(2)}) async-start(s32[32,1,4]{2,1,0:T(1,128)} %copy.73), calls=%async_computation | async-start | bytes 32768 | tf_op jit(solution)/shard_map/all_to_all | solution.py:65
  16.7 1.5 reshape.233
  18.2 7.6 %copy.78 = bf16[4096,576]{1,0:T(8,128)(2,1)} copy(bf16[4096,576]{0,1:T(8,128)(2,1)} %param.10) | data formatting | bytes 9437184 | tf_op args[0]
  25.9 9.9 %reshape.228 = bf16[64,36864]{1,0:T(8,128)(2,1)} reshape(bf16[4096,576]{1,0:T(8,128)(2,1)} %copy.78) | data formatting | bytes 9437184 | tf_op jit(solution)/shard_map/reshape | solution.py:68
  36.4 3.2 gather_fusion.2
  39.6 2.7 reshape.258
  42.4 2.5 select_select_fusion.1
  44.8 7.6 %all-to-all-start.2 = ((bf16[32,4,8192]{2,1,0:T(4,128)(2,1)}), bf16[32,4,8192]{2,1,0:T(4,128)(2,1)S(1)}, u32[]{:S(2)}, u32[]{:S(2)}) async-start(bf16[32,4,8192]{2,1,0:T(4,128)(2,1)} %select_select_fusion.1), calls=%async_computation.2 | async-start | bytes 4194304 | tf_op jit(solution)/shard_map/all_to_all | solution.py:75
  52.4 21.4 %gather_fusion = bf16[128,36864]{1,0:T(8,128)(2,1)} fusion(bf16[64,36864]{1,0:T(8,128)(2,1)} %reshape.228, s32[1024]{0:T(1024)S(1)} %pad_clamp_fusion.1), kind=kCustom, calls=%fused_computation | custom fusion | bytes 18874880 | tf_op jit(solution)/shard_map/jit(_take)/gather | solution.py:71
  73.8 13.7 %reshape.242 = bf16[32,4,36864]{2,1,0:T(4,128)(2,1)} reshape(bf16[128,36864]{1,0:T(8,128)(2,1)} %gather_fusion) | data formatting | bytes 18874368 | tf_op jit(solution)/shard_map/jit(_take)/gather | solution.py:71
  87.5 9.3 %select_select_fusion = bf16[32,4,36864]{2,1,0:T(4,128)(2,1)} fusion(bf16[32,4,36864]{2,1,0:T(4,128)(2,1)} %reshape.242, pred[32,4]{1,0:T(8,128)(4,1)S(1)} %copy.77, pred[32,4]{1,0:T(8,128)(4,1)S(1)} %copy.75), kind=kLoop, calls=%fused_computation.54 | loop fusion | flops 9437184 | bytes 18874624 | tf_op jit(solution)/shard_map/jit(_where)/select_n | solution.py:71
  96.8 1.4 copy-done
  98.2 7.4 %all-to-all-start.1 = ((bf16[32,4,36864]{2,1,0:T(4,128)(2,1)}), bf16[32,4,36864]{2,1,0:T(4,128)(2,1)}, u32[]{:S(2)}, u32[]{:S(2)}) async-start(bf16[32,4,36864]{2,1,0:T(4,128)(2,1)} %select_select_fusion), calls=%async_computation.1 | async-start | bytes 18874368 | tf_op jit(solution)/shard_map/all_to_all | solution.py:74
  106.4 4.9 copy.71
  112.1 2.5 reshape.234
  114.6 1.2 gather_fusion.3
  115.9 0.5 gather.25
  116.4 1.2 broadcast_select_fusion.1
  117.6 99.8 %all-to-all-done.1 = bf16[32,4,36864]{2,1,0:T(4,128)(2,1)} async-done(((bf16[32,4,36864]{2,1,0:T(4,128)(2,1)}), bf16[32,4,36864]{2,1,0:T(4,128)(2,1)}, u32[]{:S(2)}, u32[]{:S(2)}) %all-to-all-start.1) | async-done | bytes 9437216 | tf_op jit(solution)/shard_map/all_to_all | solution.py:74
  217.5 13.2 %reshape.229 = bf16[128,36864]{1,0:T(8,128)(2,1)} reshape(bf16[32,4,36864]{2,1,0:T(4,128)(2,1)} %all-to-all-done.1) | data formatting | bytes 18874368 | tf_op jit(solution)/shard_map/reshape | solution.py:80
  230.7 14.6 %gather_fusion.1 = bf16[64,36864]{1,0:T(8,128)(2,1)} fusion(bf16[128,36864]{1,0:T(8,128)(2,1)} %reshape.229, s32[1024]{0:T(1024)S(1)} %pad_clamp_fusion), kind=kCustom, calls=%fused_computation.1 | custom fusion | bytes 9437440 | tf_op jit(solution)/shard_map/jit(_take)/gather | solution.py:79
  245.2 9.9 %gather.22 = bf16[2,2048,576]{2,1,0:T(8,128)(2,1)} reshape(bf16[64,36864]{1,0:T(8,128)(2,1)} %gather_fusion.1) | data formatting | bytes 9437184 | tf_op jit(solution)/shard_map/jit(_take)/gather | solution.py:79
  255.1 6.5 %broadcast_select_fusion = bf16[2,2048,576]{2,1,0:T(8,128)(2,1)} fusion(bf16[2,2048,576]{2,1,0:T(8,128)(2,1)} %gather.22, pred[2,2048]{1,0:T(4,128)(4,1)S(1)} %broadcast_in_dim.176), kind=kLoop, calls=%fused_computation.55 | loop fusion | flops 2359296 | bytes 9441280 | tf_op jit(solution)/shard_map/jit(_take)/select_n | solution.py:79
  261.6 7.7 %copy.83 = bf16[2,2048,576]{1,2,0:T(8,128)(2,1)} copy(bf16[2,2048,576]{2,1,0:T(8,128)(2,1)} %broadcast_select_fusion) | data formatting | bytes 9437184 | tf_op jit(solution)/shard_map/while | solution.py:120
  269.6 43.4 %while.26 = (s32[]{:T(128)}, f32[2,64,2048]{2,1,0:T(8,128)S(1)}, f32[2,64,2048]{2,1,0:T(8,128)S(1)}, pred[2,64,2048]{2,1,0:T(8,128)(4,1)S(1)}, bf16[2,64,16,576]...) while((s32[]{:T(128)}, f32[2,64,2048]{2,1,0:T(8,128)S(1)}, ...), condition=%wide.region_7.8_spmd, body=%wide.region_2.0_spmd.sunk | while | flops 2704020480 | bytes 42652812 | solution.py:120
  269.6 8.7 %fusion.70 = f32[64,16,2048]{2,1,0:T(8,128)} fusion(bf16[2,2048,576]{1,2,0:T(8,128)(2,1)} %get-tuple-element.350, s32[]{:T(128)} %get-tuple-element.335, bf16[2,64,16,576]{3,2,1,0:T(8,128)(2,1)} %get-tuple-element.349), kind=kOutput, calls=%fused_computation.14.clone.1 | convolution fusion | flops 2415919104 | bytes 12059648 | tf_op jit(solution)/shard_map/while/body/eval_jaxpr/qhl,kl->qhk/dot_general | solution.py:100
  278.3 8.8 %select_reduce_fusion.6 = (f32[64,16]{1,0:T(8,128)S(1)}, f32[64,16,2048]{2,1,0:T(8,128)S(1)}) fusion(pred[64,2048]{1,0:T(8,128)(4,1)S(1)} %dynamic-slice_bitcast_fusion.2, f32[64,16,2048]{2,1,0:T(8,128)} %fusion.70), kind=kOutput, calls=%fused_computation.7.clone.1 | output fusion | flops 10487807 | bytes 16912384 | tf_op jit(solution)/shard_map/while/body/eval_jaxpr/sub | solution.py:112
  287.1 2.5 select_reduce_fusion.7
  289.6 1.5 multiply_reduce_fusion.4
  291.3 8.7 %fusion.70 = f32[64,16,2048]{2,1,0:T(8,128)} fusion(bf16[2,2048,576]{1,2,0:T(8,128)(2,1)} %get-tuple-element.350, s32[]{:T(128)} %get-tuple-element.335, bf16[2,64,16,576]{3,2,1,0:T(8,128)(2,1)} %get-tuple-element.349), kind=kOutput, calls=%fused_computation.14.clone.1 | convolution fusion | flops 2415919104 | bytes 12059648 | tf_op jit(solution)/shard_map/while/body/eval_jaxpr/qhl,kl->qhk/dot_general | solution.py:100
  300.0 8.8 %select_reduce_fusion.6 = (f32[64,16]{1,0:T(8,128)S(1)}, f32[64,16,2048]{2,1,0:T(8,128)S(1)}) fusion(pred[64,2048]{1,0:T(8,128)(4,1)S(1)} %dynamic-slice_bitcast_fusion.2, f32[64,16,2048]{2,1,0:T(8,128)} %fusion.70), kind=kOutput, calls=%fused_computation.7.clone.1 | output fusion | flops 10487807 | bytes 16912384 | tf_op jit(solution)/shard_map/while/body/eval_jaxpr/sub | solution.py:112
  308.9 2.5 select_reduce_fusion.7
  311.4 1.5 multiply_reduce_fusion.4
  313.0 1.0 copy-done.1
  314.4 87.8 %all-reduce.3.cloned.1.call-done = (f32[2,64,2048]{2,1,0:T(8,128)}, f32[2,64,2048]{2,1,0:T(8,128)}) async-done(((f32[2,64,2048]{2,1,0:T(8,128)}, f32[2,64,2048]{2,1,0:T(8,128)}), (f32[2,64,2048]{2,1,0:T(8,128)}, f32[2,64,2048]{2,1,0:T(8,128)})) %all-reduce.3.cloned.1.call-update) | async-done | bytes 2097168 | tf_op jit(solution)/shard_map/psum | solution.py:123
  402.2 1.5 fusion.34
  403.8 2.1 fusion.39
  405.9 10.6 %while.27 = (s32[]{:T(128)}, f32[2,64,8]{2,1,0:T(8,128)S(1)}, f32[2,64,8,128]{3,2,1,0:T(8,128)}, f32[2,2048,128]{2,1,0:T(8,128)}, bf16[2,64,2048]{2,1,0:T(8,128)...) while((s32[]{:T(128)}, f32[2,64,8]{2,1,0:T(8,128)S(1)}, ...), condition=%wide.region_16.17_spmd, body=%wide.region_14.16_spmd.sunk | while | flops 822214656 | bytes 38674648 | solution.py:148
  406.1 0.9 multiply_reduce_fusion.5
  407.1 0.6 copy-done.3
  407.6 1.4 fusion.74
  409.1 1.0 fusion.73
  410.5 0.8 copy-done.12
  411.3 0.9 multiply_reduce_fusion.5
  412.2 0.6 copy-done.3
  412.8 1.4 fusion.74
  414.3 1.0 fusion.73
  415.6 0.8 copy-done.12
  416.4 1.7 reshape.277
  418.2 4.0 scatter_custom_fusion
  422.2 2.6 convert_bitcast_fusion
  424.7 1.9 copy.88
  426.7 7.4 %all-to-all-start.3 = ((bf16[32,4,64,128]{3,2,1,0:T(8,128)(2,1)}), bf16[32,4,64,128]{3,2,1,0:T(8,128)(2,1)S(1)}, u32[]{:S(2)}, u32[]{:S(2)}) async-start(bf16[32,4,64,128]{3,2,1,0:T(8,128)(2,1)} %bitcast.119), calls=%async_computation.3 | async-start | bytes 4194304 | tf_op jit(solution)/shard_map/all_to_all | solution.py:154
  434.7 0.7 reduce.3
  435.5 26.5 %all-to-all-done.3 = bf16[32,4,64,128]{3,2,1,0:T(8,128)(2,1)S(1)} async-done(((bf16[32,4,64,128]{3,2,1,0:T(8,128)(2,1)}), bf16[32,4,64,128]{3,2,1,0:T(8,128)(2,1)S(1)}, u32[]{:S(2)}, u32[]{:S(2)}) %all-to-all-start.3) | async-done | bytes 2097184 | tf_op jit(solution)/shard_map/all_to_all | solution.py:154
  462.0 3.2 copy.91
  465.1 3.2 copy.85
  468.4 1.8 convolution_convert_fusion
  470.2 0.7 copy.87
  471.0 0.6 dynamic_slice.40
  471.6 34.2 %reduce-scatter.2.cloned.1.call-done = bf16[64,8,128]{2,0,1:T(8,128)(2,1)} async-done(((bf16[64,64,128]{2,0,1:T(8,128)(2,1)}), bf16[64,8,128]{2,0,1:T(8,128)(2,1)}) %reduce-scatter.2.cloned.1.call-update) | async-done | bytes 131088 | tf_op jit(solution)/shard_map/reduce_scatter | solution.py:165
  505.8 1.7 copy.86
  (89 shorter events, 5.0 us)
Async XLA Ops:
  9.1 26.7 %all-to-all-start = ((s32[32,1,4]{2,1,0:T(1,128)}), s32[32,1,4]{2,1,0:T(1,128)S(1)}, u32[]{:S(2)}, u32[]{:S(2)}) async-start(s32[32,1,4]{2,1,0:T(1,128)} %copy.73), calls=%async_computation | async-start | bytes 32768 | tf_op jit(solution)/shard_map/all_to_all | solution.py:65
  35.8 0.6 copy-start.7
  44.8 52.0 %all-to-all-start.2 = ((bf16[32,4,8192]{2,1,0:T(4,128)(2,1)}), bf16[32,4,8192]{2,1,0:T(4,128)(2,1)S(1)}, u32[]{:S(2)}, u32[]{:S(2)}) async-start(bf16[32,4,8192]{2,1,0:T(4,128)(2,1)} %select_select_fusion.1), calls=%async_computation.2 | async-start | bytes 4194304 | tf_op jit(solution)/shard_map/all_to_all | solution.py:75
  96.8 9.5 %copy-start.9 = (bf16[128,8]{0,1:T(8,128)(2,1)S(1)}, bf16[128,8]{0,1:T(8,128)(2,1)}, u32[]{:S(2)}) copy-start(bf16[128,8]{0,1:T(8,128)(2,1)} %param.14) | copy-start | bytes 6148
  96.8 1.4 copy-start
  98.2 119.2 %all-to-all-start.1 = ((bf16[32,4,36864]{2,1,0:T(4,128)(2,1)}), bf16[32,4,36864]{2,1,0:T(4,128)(2,1)}, u32[]{:S(2)}, u32[]{:S(2)}) async-start(bf16[32,4,36864]{2,1,0:T(4,128)(2,1)} %select_select_fusion), calls=%async_computation.1 | async-start | bytes 18874368 | tf_op jit(solution)/shard_map/all_to_all | solution.py:74
  105.7 296.6 %all-reduce.3.cloned.1.call-start = ((), (), s32[]{:S(2)}) async-start(), calls=%async_computation.6 | async-start | bytes 4194304 | tf_op jit(solution)/shard_map/psum | solution.py:123
  111.4 0.5 copy-start.10
  287.1 2.5 copy-start.5
  308.8 2.5 copy-start.5
  313.0 1.0 copy-start.1
  313.0 1.3 copy-start.2
  314.3 91.5 %copy-start.6 = (bf16[2,64,8,128]{3,2,1,0:T(8,128)(2,1)S(1)}, bf16[2,64,8,128]{3,2,1,0:T(8,128)(2,1)}, u32[]{:S(2)}) copy-start(bf16[2,64,8,128]{3,2,1,0:T(8,128)(2,1)} %get-tuple-element.401) | copy-start | bytes 786436
  406.1 1.6 copy-start.3
  407.6 1.5 copy-start.11
  409.1 1.4 copy-start.4
  410.4 0.8 copy-start.12
  411.2 1.6 copy-start.3
  412.8 1.5 copy-start.11
  414.3 1.4 copy-start.4
  415.6 0.8 copy-start.12
  424.7 9.9 %copy-start.8 = (s32[32,1,4]{2,1,0:T(1,128)S(1)}, s32[32,1,4]{2,1,0:T(1,128)}, u32[]{:S(2)}) copy-start(s32[32,1,4]{2,1,0:T(1,128)} %copy-done.7) | copy-start | bytes 1540
  426.7 35.3 %all-to-all-start.3 = ((bf16[32,4,64,128]{3,2,1,0:T(8,128)(2,1)}), bf16[32,4,64,128]{3,2,1,0:T(8,128)(2,1)S(1)}, u32[]{:S(2)}, u32[]{:S(2)}) async-start(bf16[32,4,64,128]{3,2,1,0:T(8,128)(2,1)} %bitcast.119), calls=%async_computation.3 | async-start | bytes 4194304 | tf_op jit(solution)/shard_map/all_to_all | solution.py:154
  434.1 71.7 %reduce-scatter.2.cloned.1.call-start = ((), (), s32[]{:S(2)}) async-start(), calls=%async_computation.5 | async-start | bytes 1179648 | tf_op jit(solution)/shard_map/reduce_scatter | solution.py:165
Sparse Core Ops, SparseCore 0:
  314.5 87.7 all-reduce.2
  470.3 35.3 reduce-scatter.1
where the time goes:
time: 521 us; the launch traced here: 515 us
  waiting for transfers between devices  248 us (48%)
  local copies, waits for them, and re-layouts  141 us (27%)
  other arithmetic  50.5 us (10%)
  starting transfers between devices  30.1 us (6%)
  matrix products  28.9 us (6%)
  between operations  14.6 us (3%)
    all_to_all x1, waiting for transfers between devices, local(): lax.all_to_all(lat_out, 'ctx', split_axis=0, concat_axis=0, tiled=True)  99.8 us
    psum x1, waiting for transfers between devices, local(): target, logits = lax.psum((target_part, logit_part), 'head')  87.8 us
    gather x2, local copies, waits for them, and re-layouts, local(): jnp.take(lat_table, safe_ids, axis=0)  35.1 us
    reduce_scatter x1, waiting for transfers between devices, local(): lax.psum_scatter(summed.astype(jnp.bfloat16), 'head', scatter_dimension=1...  34.2 us
    all_to_all x1, waiting for transfers between devices, local(): lax.all_to_all(slot_grads.astype(jnp.bfloat16), 'ctx', split_axis=0, conc...  26.5 us
    gather x2, local copies, waits for them, and re-layouts, local(): jnp.take(lat_back.reshape(ctx_count * slot_count, BLK * LAT), flat_slot,...  24.4 us
    unnamed x22, local copies, waits for them, and re-layouts  22.7 us
    sub x2, other arithmetic, forward_block(): raw_scores - peak  17.7 us
  transfers between devices with their start and end apart: 6, of which 4 were waited for; matrix products, arithmetic and copies ran while one was open for 15% of the time, Pallas kernels for 0%

commit v1 on v0

v1 whole, which is shorter than its diff:
```python
import functools
import math

import jax
import jax.numpy as jnp
from jax import lax
from jax.experimental import pallas as pl
from jax.experimental.pallas import tpu as pltpu
from jax.sharding import PartitionSpec as P

MESH = pl.DeviceIdType.MESH
LAT, DI, BLK, SEL = 576, 128, 64, 32
HEADS = 128
NZ, SIDE = 8, 4
NCOL = SIDE * SIDE
NCTX = 2 * NCOL
CONTEXT, QUERIES = 131072, 4096
SPAN = SEL * BLK
EXT = 640
WIDE = EXT + DI
FLOOR = -1e30
LOW = -2e30
BIG = 1 << 28
EXP_SCALE = 192.0**-0.5 * math.log2(math.e)
IDX_SCALE = DI**-0.5
UROWS = 512
F32, BF16, I32 = jnp.float32, jnp.bfloat16, jnp.int32

OFFSETS = [(0, 0)] + sorted(
    [(i // SIDE, i % SIDE) for i in range(1, NCOL)], key=lambda o: -((o[0] == 2) + (o[1] == 2))
)
CODES = [dy * SIDE + dx for dy, dx in OFFSETS]


def pick(index, values):
    out = values[0]
    for i in range(1, len(values)):
        out = jnp.where(index == i, values[i], out)
    return out


def nt(a, b):
    return lax.dot_general(a, b, (((1,), (1,)), ((), ())), preferred_element_type=F32)


def kernel(
    sel_in, lat_hbm, ik_hbm, mq_hbm, iq_hbm, iw_in,
    gk_out, gq_out, gw_out, kl_out,
    lat, ikv, selall, tbl, tbs, stage, rs, qbuf, qx, prob, mrun, zrun, mchunk, wts, xbuf,
    iq, iqt, iw, wcol, ikc, kpos, tq, tqb, tsib, tfar, fac, gwacc, gkf, gsend, grecv, kz, kr, kc,
    pm, pr, gqm, gqr, klm, klr,
    ld_s, sel_s, sel_r, tb_s, q_s, q_r, iq_s, iq_r, iw_s, iw_r, st_s, st_r, fw_s, fw_r,
    ts_s, ts_r, tf_s, tf_r, gs_s, gs_r, kz_s, kz_r, pm_s, pm_r, gq_s, gq_r, kl_s, kl_r,
):
    me = lax.axis_index("ctx")
    z = lax.axis_index("head")
    k, core = me // 2, me % 2
    ky, kx = k // SIDE, k % SIDE
    sib = 2 * k + 1 - core
    rho = z % 4
    half = z // 4
    src_ctx = 2 * k + rho // 2
    blk_b = rho % 2
    t_own = 2 * half + core

    def column(code, sign):
        dy, dx = code // SIDE, code % SIDE
        return ((ky + sign * dy + SIDE) % SIDE) * SIDE + (kx + sign * dx + SIDE) % SIDE

    def send(src, dst, ssem, rsem, ctx, head):
        own = jnp.logical_and(ctx == me, head == z)
        remote = pltpu.make_async_remote_copy(
            src, dst, ssem, rsem, device_id={"ctx": ctx, "head": head}, device_id_type=MESH
        )

        @pl.when(own)
        def _():
            pltpu.make_async_copy(src, dst, rsem).start()

        @pl.when(jnp.logical_not(own))
        def _():
            remote.start()

        def finish():
            @pl.when(jnp.logical_not(own))
            def _():
                remote.wait_send()

        return finish

    def remote(src, dst, ssem, rsem, ctx, head):
        return pltpu.make_async_remote_copy(
            src, dst, ssem, rsem, device_id={"ctx": ctx, "head": head}, device_id_type=MESH
        )

    def arrived(dst, rsem):
        pltpu.make_async_copy(dst, dst, rsem).wait()

    pending = []

    load_lat = pltpu.make_async_copy(lat_hbm, lat, ld_s.at[0])
    load_ik = pltpu.make_async_copy(ik_hbm, ikv, ld_s.at[1])
    load_lat.start()
    load_ik.start()
    barrier = pltpu.get_barrier_semaphore()

    def greet_plane(d, carry):
        pl.semaphore_signal(
            barrier, inc=1, device_id={"ctx": (me + d) % NCTX, "head": z}, device_id_type=MESH
        )
        return carry

    def greet_column(d, carry):
        for c in range(2):
            pl.semaphore_signal(
                barrier, inc=1, device_id={"ctx": 2 * k + c, "head": (z + d) % NZ}, device_id_type=MESH
            )
        return carry

    lax.fori_loop(1, NCTX, greet_plane, 0)
    lax.fori_loop(1, NZ, greet_column, 0)
    selall[pl.ds(me, 1), 0:2, 0:SEL] = sel_in[...].reshape(1, 2, SEL)
    pl.semaphore_wait(barrier, NCTX - 1 + 2 * (NZ - 1))

    def sel_copy(d):
        return remote(
            selall.at[me], selall.at[me], sel_s.at[d], sel_r.at[me], (me + d) % NCTX, z
        )

    def sel_start(d, carry):
        sel_copy(d).start()
        return carry

    lax.fori_loop(1, NCTX, sel_start, 0)

    for b in range(2):
        r = 2 * core + b
        d = (r - z + 8) % 4
        for hq in range(2):
            dz = pick(d, [0, 1, 2, 7] if hq == 0 else [0, 1, 6, 7])
            tcore = pick(d, [0, 0, 0, 1] if hq == 0 else [1, 0, 1, 1])
            unit = pick(d, [0, 1, 3, 1] if hq == 0 else [0, 2, 3, 2])
            pending.append(
                send(
                    mq_hbm.at[pl.ds(BLK * b + 32 * hq, 32)], qbuf.at[unit],
                    q_s.at[2 * b + hq], q_r.at[unit], 2 * k + tcore, (z + dz) % NZ,
                )
            )
    for b in range(2):
        for t in range(4):
            tz = 2 * core + b + 4 * (t // 2)
            tc = 2 * k + t % 2
            pending.append(
                send(
                    iq_hbm.at[pl.ds((BLK * b + 16 * t) * 8, 128)], iq.at[z],
                    iq_s.at[4 * b + t], iq_r.at[z], tc, tz,
                )
            )
            pending.append(
                send(
                    iw_in.at[pl.ds(BLK * b + 16 * t, 16)], iw.at[z],
                    iw_s.at[4 * b + t], iw_r.at[z], tc, tz,
                )
            )

    def sel_wait(d, carry):
        src = (me + d) % NCTX
        arrived(selall.at[src], sel_r.at[src])
        return carry

    lax.fori_loop(1, NCTX, sel_wait, 0)
    lane = lax.broadcasted_iota(I32, (NCTX, 128), 1)
    sub = lax.broadcasted_iota(I32, (NCTX, 128), 0)
    lane_f = lane.astype(F32)
    sub3 = lax.broadcasted_iota(I32, (NCTX, 8, 128), 1)

    def rows_of(b):
        return jnp.sum(jnp.where(sub3 == b, selall[...], 0).astype(F32), axis=1).astype(I32)

    def two(match, values):
        first = jnp.min(jnp.where(match, lane_f, 128.0), axis=1, keepdims=True)
        hit0 = jnp.logical_and(match, lane_f == first)
        hit1 = jnp.logical_and(match, lane_f > first)
        second = jnp.min(jnp.where(hit1, lane_f, 128.0), axis=1, keepdims=True)
        v0 = jnp.sum(jnp.where(hit0, values, 0.0), axis=1, keepdims=True)
        v1 = jnp.sum(jnp.where(hit1, values, 0.0), axis=1, keepdims=True)
        return first, second, v0, v1

    def lanes(columns):
        out = jnp.zeros((NCTX, 128), F32)
        for i, c in enumerate(columns):
            out = jnp.where(lane == i, c, out)
        return out

    listed = lane < SEL
    wanted = []
    for b in range(2):
        rows = rows_of(b)
        match = jnp.logical_and(listed, rows // BLK == me)
        _, _, v0, v1 = two(match, (rows % BLK + 1).astype(F32))
        wanted += [v0 - 1.0, v1 - 1.0]
    table1 = lanes(wanted)
    tbl[0:NCTX, :] = table1.astype(I32)

    sub8 = lax.broadcasted_iota(I32, (8, 128), 0)

    def row_of(ctx, b):
        tile = selall[pl.ds(ctx, 1)].reshape(8, 128)
        return jnp.sum(jnp.where(sub8 == b, tile, 0).astype(F32), axis=0, keepdims=True)

    def by_owner(row):
        row = jnp.broadcast_to(row.astype(I32), (NCTX, 128))
        match = jnp.logical_and(listed, row // BLK == sub)
        return match, two(match, row.astype(F32) + 1.0)

    my_row = row_of(src_ctx, blk_b)
    match, (first, second, v0, v1) = by_owner(my_row)
    base0 = jnp.where(v0 > 0.5, (v0 - 1.0) * BLK, float(BIG))
    base1 = jnp.where(v1 > 0.5, (v1 - 1.0) * BLK, float(BIG))
    owner_col = sub // 2
    code = ((ky - owner_col // SIDE + SIDE) % SIDE) * SIDE + (kx - owner_col % SIDE + SIDE) % SIDE
    place = jnp.zeros_like(code)
    for i, c in enumerate(CODES):
        place = jnp.where(code == c, i, place)
    slot = (place * 4 + (sub % 2) * 2).astype(F32) + jnp.where(lane_f == first, 0.0, 1.0)
    slots = jnp.sum(jnp.where(match, slot, 0.0), axis=0, keepdims=True)
    columns = [base0, base1]
    for b in range(2):
        _, (f, s, _, _) = by_owner(row_of(me, b))
        columns += [jnp.minimum(f, float(SEL)), jnp.minimum(s, float(SEL))]
    tbl[NCTX : 2 * NCTX, :] = lanes(columns).astype(I32)
    tbl[2 * NCTX : 2 * NCTX + 8, :] = jnp.where(
        sub8 == 0, jnp.broadcast_to(slots, (8, 128)), jnp.broadcast_to(my_row, (8, 128))
    ).astype(I32)
    to_smem = pltpu.make_async_copy(tbl, tbs, tb_s.at[0])
    to_smem.start()
    to_smem.wait()
    load_lat.wait()
    load_ik.wait()

    def gather(code, put):
        ctx = 2 * column(code, 1) + rho // 2
        for r in range(2):
            index = jnp.clip(tbs[ctx, 2 * blk_b + r], 0, BLK - 1)
            rows = lat[pl.ds(index, 1)].reshape(BLK, LAT)
            tail = jnp.concatenate(
                [rows[:, 512:LAT], jnp.zeros((BLK, EXT - LAT), BF16)], axis=1
            )
            put(r, rows[:, 0:512], tail, ikv[pl.ds(index, 1)].reshape(BLK, DI))

    def put_own(r, head, tail, keys):
        rs[0, core, r, :, 0:512] = head
        rs[0, core, r, :, 512:EXT] = tail
        rs[0, core, r, :, EXT:WIDE] = keys

    def stage_copy(i):
        to = 2 * column(pick(i, CODES), 1) + core
        return remote(stage.at[i], rs.at[i, core], st_s.at[i], st_r.at[i], to, z)

    def stage_send(i, carry):
        def put(r, head, tail, keys):
            stage[i, r, :, 0:512] = head
            stage[i, r, :, 512:EXT] = tail
            stage[i, r, :, EXT:WIDE] = keys

        gather(pick(i, CODES), put)
        stage_copy(i).start()
        return carry

    lax.fori_loop(1, NCOL, stage_send, 0)
    gather(0, put_own)

    def forward_copy(i):
        return remote(rs.at[i, core], rs.at[i, core], fw_s.at[i], fw_r.at[i], sib, z)

    key_off = lax.broadcasted_iota(I32, (BLK, 128), 0)
    lane_q = lax.broadcasted_iota(I32, (BLK, 128), 1)
    q_base = CONTEXT - QUERIES + src_ctx * 128 + blk_b * BLK
    reach = lane_q - BLK + q_base - key_off

    def forward(c):
        for e in range(2):
            i = 2 * c + e

            @pl.when(i > 0)
            def _():
                arrived(rs.at[i, core], st_r.at[i])

            forward_copy(i).start()

    def settle(c):
        for e in range(2):
            i = 2 * c + e
            arrived(rs.at[i, 1 - core], fw_r.at[i])
            forward_copy(i).wait_send()
            owner_k = column(pick(i, CODES), -1)
            for oc in range(2):
                for r in range(2):
                    base = tbs[NCTX + 2 * owner_k + oc, r]
                    old = rs[i, oc, r, :, 512:EXT].astype(F32)
                    bias = jnp.where(base > reach, FLOOR, 0.0)
                    rs[i, oc, r, :, 512:EXT] = jnp.where(lane_q < BLK, old, bias).astype(BF16)

    def query_unit(u):
        arrived(qbuf.at[u], q_r.at[u])
        v = qbuf[u].reshape(UROWS, LAT)
        first_q = pick(u, [32 * core, 0, 32, 32 * core])
        row = lax.broadcasted_iota(I32, (UROWS, 64), 0) // 16 + first_q
        col = lax.broadcasted_iota(I32, (UROWS, 64), 1)
        hot = jnp.where(row == col, 1.0, 0.0).astype(BF16)
        qx[u, :, 0:512] = v[:, 0:512]
        qx[u, :, 512:EXT] = jnp.concatenate([v[:, 512:LAT], hot], axis=1)
        mrun[u] = jnp.full((1, UROWS), LOW, F32)
        zrun[u] = jnp.zeros((1, UROWS), F32)

    def pair(u, c):
        keys = rs[pl.ds(2 * c, 2), :, :, :, 0:EXT].reshape(512, EXT)
        s = nt(keys, qx[u])
        old = mrun[u]
        new = jnp.maximum(old, jnp.max(s, axis=0, keepdims=True))
        p = jnp.exp2((s - new) * EXP_SCALE)
        zrun[u] = zrun[u] * jnp.exp2((old - new) * EXP_SCALE) + jnp.sum(p, axis=0, keepdims=True)
        mrun[u] = new
        mchunk[c, u] = new
        prob[c, u] = p.astype(BF16).reshape(8, BLK, UROWS)

    def pairs(us, cs):
        n = len(us)
        u0, c0 = us[0], cs[0]

        def step(i, carry):
            pair(u0 + i % n, c0 + i // n)
            return carry

        lax.fori_loop(0, n * len(cs), step, 0)

    def chunks(us, first_c, last_c):
        def step(c, carry):
            forward(c)

            def inner(u, carry2):
                pair(u, c - 1)
                return carry2

            lax.fori_loop(us[0], us[-1] + 1, inner, 0)
            settle(c)
            return carry

        lax.fori_loop(first_c, last_c, step, 0)

    query_unit(0)
    forward(0)
    settle(0)
    chunks([0], 1, 4)
    for u in (1, 2):
        query_unit(u)
    pairs([1, 2], [0, 1, 2])
    chunks([0, 1, 2], 4, 6)
    query_unit(3)
    pairs([3], [0, 1, 2, 3, 4])
    chunks([0, 1, 2, 3], 6, 8)
    pairs([0, 1, 2, 3], [7])

    for u in range(4):
        scale = 1.0 / (zrun[u] * HEADS)
        for c in range(8):
            wts[c, u] = jnp.exp2((mchunk[c, u] - mrun[u]) * EXP_SCALE) * scale

    def compact(i, carry):
        s = jnp.clip(tbs[2 * NCTX, i], 0, 63)
        c, j = s // 8, s % 8

        def part(u):
            return prob[pl.ds(c, 1), pl.ds(u, 1), pl.ds(j, 1)].reshape(BLK, UROWS).astype(F32) * wts[
                pl.ds(c, 1), pl.ds(u, 1)
            ].reshape(1, UROWS)

        xbuf[0, pl.ds(i, 1)] = (part(0) + part(3) + part(1 + core)).astype(BF16).reshape(1, BLK, UROWS)
        xbuf[1, pl.ds(i, 1)] = part(2 - core).astype(BF16).reshape(1, BLK, UROWS)
        ikc[pl.ds(i, 1)] = rs[
            pl.ds(s // 4, 1), pl.ds(s // 2 % 2, 1), pl.ds(s % 2, 1), :, EXT:WIDE
        ].reshape(1, BLK, DI)
        return carry

    lax.fori_loop(0, SEL, compact, 0)
    fold = jnp.where(
        lax.broadcasted_iota(I32, (32, UROWS), 0) == lax.broadcasted_iota(I32, (32, UROWS), 1) // 16, 1.0, 0.0
    ).astype(BF16)
    for x in range(2):
        part = nt(fold, xbuf[x].reshape(SPAN, UROWS))
        h = core if x == 0 else 1 - core
        tq[pl.ds(2 * h, 2)] = part.reshape(2, 16, SPAN)
        tqb[pl.ds(2 * h, 2)] = part.astype(BF16).reshape(2, 16, SPAN)
    sib_copies = [
        remote(tqb.at[1 - core + 2 * h], tsib.at[h], ts_s.at[h], ts_r.at[h], sib, z) for h in range(2)
    ]
    for copy in sib_copies:
        copy.start()

    row_q = lax.broadcasted_iota(I32, (128, 16), 0) // 8
    spread = jnp.where(row_q == lax.broadcasted_iota(I32, (128, 16), 1), 1.0, 0.0).astype(BF16)
    row_j = lax.broadcasted_iota(I32, (128, 8), 0) % 8
    for s in range(NZ):
        arrived(iq.at[s], iq_r.at[s])
        arrived(iw.at[s], iw_r.at[s])
        w = jnp.dot(spread, iw[s], preferred_element_type=F32)
        w = jnp.sum(
            jnp.where(row_j == lax.broadcasted_iota(I32, (128, 8), 1), w, 0.0), axis=1, keepdims=True
        )
        wcol[s] = jnp.broadcast_to(w * IDX_SCALE, (128, 128))
        iqt[:, 128 * s : 128 * (s + 1)] = iq[s].astype(F32).T.astype(BF16)

    TILE = 512

    def dots_of(s, kt):
        keys = ikc[pl.ds(kt * (TILE // BLK), TILE // BLK)].reshape(TILE, DI)
        return nt(iq[s], keys)

    logit_tiles = []
    for kt in range(SPAN // TILE):
        acc = jnp.zeros((128, TILE), F32)
        for s in range(NZ):
            w = jnp.concatenate([wcol[s]] * (TILE // 128), axis=1)
            acc = acc + w * jnp.maximum(dots_of(s, kt), 0.0)
        logit_tiles.append(jnp.sum(acc.reshape(16, 8, TILE), axis=1))
    logits = jnp.concatenate(logit_tiles, axis=1)

    def positions(i, carry):
        l8 = lax.broadcasted_iota(I32, (8, 128), 1)
        a, b = tbs[2 * NCTX + 1, 2 * i] * BLK, tbs[2 * NCTX + 1, 2 * i + 1] * BLK
        kpos[pl.ds(i, 1)] = (jnp.where(l8 < BLK, a, b) + l8 % BLK).reshape(1, 8, 128)
        return carry

    lax.fori_loop(0, SPAN // 128, positions, 0)
    q_pos = q_base + 16 * t_own + lax.broadcasted_iota(I32, (16, 128), 0)
    visible = jnp.concatenate(
        [jnp.concatenate([kpos[i]] * 2, axis=0) <= q_pos for i in range(SPAN // 128)], axis=1
    )

    for h, copy in enumerate(sib_copies):
        arrived(tsib.at[h], ts_r.at[h])
        copy.wait_send()
    far = 1 - half
    mine = tq[pl.ds(2 * half + core, 1)].reshape(16, SPAN) + tsib[pl.ds(half, 1)].reshape(16, SPAN).astype(F32)
    other = tq[pl.ds(2 * far + core, 1)].reshape(16, SPAN) + tsib[pl.ds(far, 1)].reshape(16, SPAN).astype(F32)
    tfar[0] = other.astype(BF16)
    far_copy = remote(tfar.at[0], tfar.at[1], tf_s.at[0], tf_r.at[0], me, (z + 4) % NZ)
    far_copy.start()
    masked = jnp.where(visible, logits, FLOOR)
    shifted = masked - jnp.max(masked, axis=1, keepdims=True)
    log_norm = jnp.log(jnp.sum(jnp.exp(shifted), axis=1, keepdims=True))
    log_ratio = shifted - log_norm
    predicted = jnp.where(visible, jnp.exp(log_ratio), 0.0)
    arrived(tfar.at[1], tf_r.at[0])
    target = mine + tfar[1].astype(F32)
    positive = target > 0.0
    entropy = jnp.sum(
        jnp.where(positive, target * jnp.log(jnp.where(positive, target, 1.0)), 0.0), axis=1, keepdims=True
    )
    cross = jnp.sum(jnp.where(visible, target * log_ratio, 0.0), axis=1, keepdims=True)
    gradient = jnp.where(visible, SPAN * (predicted - target), 0.0).astype(BF16).astype(F32)
    divergence = entropy - cross
    spot = lax.broadcasted_iota(I32, (16, 128), 0) == lax.broadcasted_iota(I32, (16, 128), 1)
    klm[...] = jnp.broadcast_to(
        jnp.sum(jnp.where(spot, divergence, 0.0), axis=0, keepdims=True), (8, 128)
    )
    pending.append(
        send(klm, klr, kl_s.at[0], kl_r.at[0], src_ctx, 4 * blk_b + t_own)
    )

    for kt in range(SPAN // TILE):
        g = gradient[:, kt * TILE : (kt + 1) * TILE]
        g = jnp.broadcast_to(g.reshape(16, 1, TILE), (16, 8, TILE)).reshape(128, TILE)
        for s in range(NZ):
            dots = dots_of(s, kt)
            weighted = g * jnp.maximum(dots, 0.0)
            lanesum = weighted[:, 0:128]
            for i in range(1, TILE // 128):
                lanesum = lanesum + weighted[:, 128 * i : 128 * (i + 1)]
            gwacc[s] = lanesum if kt == 0 else gwacc[s] + lanesum
            w = jnp.concatenate([wcol[s]] * (TILE // 128), axis=1)
            fac[128 * s : 128 * (s + 1), kt * TILE : (kt + 1) * TILE] = jnp.where(
                dots > 0.0, g * w, 0.0
            ).astype(BF16)
    unspread = jnp.where(
        lax.broadcasted_iota(I32, (16, 128), 0) == lax.broadcasted_iota(I32, (16, 128), 1) // 8, 1.0, 0.0
    )
    diag_j = lax.broadcasted_iota(I32, (128, 128), 0) % 8 == lax.broadcasted_iota(I32, (128, 128), 1)
    for s in range(NZ):
        gq = jnp.dot(
            fac[128 * s : 128 * (s + 1), :], ikc[...].reshape(SPAN, DI), preferred_element_type=F32
        )
        gqm[s, 0:128, :] = gq.astype(BF16)
        gw = jnp.sum(gwacc[s], axis=1, keepdims=True) * IDX_SCALE
        gw = jnp.dot(
            unspread, jnp.where(diag_j, gw, 0.0), preferred_element_type=F32, precision=lax.Precision.HIGHEST
        )
        gqm[s, 128:144, :] = gw.astype(BF16)
        pending.append(
            send(
                gqm.at[s], gqr.at[4 * blk_b + t_own], gq_s.at[s], gq_r.at[4 * blk_b + t_own], src_ctx, s
            )
        )
    for kt in range(SPAN // TILE):
        part = jnp.dot(
            iqt[...], fac[:, kt * TILE : (kt + 1) * TILE], preferred_element_type=F32
        )
        gkf[kt * (TILE // BLK) : (kt + 1) * (TILE // BLK)] = part.T.reshape(TILE // BLK, BLK, DI)

    gsend[...] = gkf[:, pl.ds(32 * (1 - core), 32), :].astype(BF16)
    swap = remote(gsend, grecv, gs_s.at[0], gs_r.at[0], sib, z)
    swap.start()
    arrived(grecv, gs_r.at[0])
    both = gkf[:, pl.ds(32 * core, 32), :] + grecv[...].astype(F32)
    for t in range(4):
        kz[t] = both[:, 8 * t : 8 * t + 8, :].reshape(SEL * 8, DI).astype(BF16)
        pending.append(
            send(
                kz.at[t], kr.at[2 * blk_b + half], kz_s.at[t], kz_r.at[2 * blk_b + half],
                src_ctx, 4 * core + t,
            )
        )
    swap.wait_send()
    for b in range(2):
        for h in range(2):
            arrived(kr.at[2 * b + h], kz_r.at[2 * b + h])
        total = kr[2 * b].astype(F32) + kr[2 * b + 1].astype(F32)
        kc[b, 0:SEL] = total.reshape(SEL, 8, DI)
        kc[b, SEL : SEL + 1] = jnp.zeros((1, 8, DI), F32)

    def owner_copy(o):
        return remote(pm.at[o], pr.at[me], pm_s.at[o], pm_r.at[me], o, z)

    def owner_block(o):
        parts = []
        for b in range(2):
            for r in range(2):
                index = jnp.clip(tbs[NCTX + o, 2 + 2 * b + r], 0, SEL)
                parts.append(kc[pl.ds(b, 1), pl.ds(index, 1)].reshape(8, DI))
        return jnp.concatenate(parts, axis=0).astype(BF16)

    def owner_of(i):
        return 2 * column(pick(i // 2, CODES), 1) + (core + i) % 2

    def owner_send(i, carry):
        o = owner_of(i)
        pm[pl.ds(o, 1)] = owner_block(o).reshape(1, 32, DI)
        owner_copy(o).start()
        return carry

    lax.fori_loop(1, NCTX, owner_send, 0)
    pr[pl.ds(me, 1)] = owner_block(me).reshape(1, 32, DI)

    col = lax.broadcasted_iota(I32, (128, 1024), 1)
    expand = jnp.where(col % 32 // 8 == lax.broadcasted_iota(I32, (128, 1024), 0), 1.0, 0.0).astype(BF16)
    wide = jnp.dot(table1.astype(BF16), expand, preferred_element_type=F32)
    col = lax.broadcasted_iota(I32, (NCTX, 1024), 1)
    wide = jnp.where(col // 32 == lax.broadcasted_iota(I32, (NCTX, 1024), 0), wide * 8.0, 0.0)
    code = jnp.sum(wide, axis=0, keepdims=True) + (
        lax.broadcasted_iota(I32, (1, 1024), 1) % 8
    ).astype(F32)
    row = lax.broadcasted_iota(I32, (512, 1024), 0).astype(F32)
    hot = jnp.where(row == code, 1.0, 0.0).astype(BF16)

    arrived(klr, kl_r.at[0])
    kl_out[...] = klr[0:1, :]
    for i in range(8):
        arrived(gqr.at[i], gq_r.at[i])
        gq_out[128 * i : 128 * (i + 1), :] = gqr[i, 0:128, :].astype(F32)
        gw_out[16 * i : 16 * (i + 1), :] = gqr[i, 128:144, 0:8].astype(F32)

    def owner_wait(i, carry):
        o = owner_of(i)
        arrived(pr.at[o], pm_r.at[o])
        owner_copy(o).wait_send()
        return carry

    lax.fori_loop(1, NCTX, owner_wait, 0)
    gk_out[...] = jnp.dot(hot, pr[...].reshape(1024, DI), preferred_element_type=F32)

    for finish in pending:
        finish()
    far_copy.wait_send()

    def drain_sel(d, carry):
        sel_copy(d).wait_send()
        return carry

    def drain_stage(i, carry):
        stage_copy(i).wait_send()
        return carry

    lax.fori_loop(1, NCTX, drain_sel, 0)
    lax.fori_loop(1, NCOL, drain_stage, 0)


def local(latents, idx_keys, mla_query, idx_query, idx_weight, sel_blocks):
    V = pltpu.VMEM
    dma = pltpu.SemaphoreType.DMA
    hbm = pl.BlockSpec(memory_space=pl.ANY)
    vmem = pl.BlockSpec(memory_space=pltpu.VMEM)
    scratch = [
        V((BLK, BLK, LAT), BF16), V((BLK, BLK, DI), BF16), V((NCTX, 8, 128), I32),
        V((2 * NCTX + 8, 128), I32), pltpu.SMEM((2 * NCTX + 8, 128), I32),
        V((NCOL, 2, BLK, WIDE), BF16), V((NCOL, 2, 2, BLK, WIDE), BF16),
        V((4, 32, 16, LAT), BF16), V((4, UROWS, EXT), BF16),
        V((8, 4, 8, BLK, UROWS), BF16), V((4, 1, UROWS), F32), V((4, 1, UROWS), F32),
        V((8, 4, 1, UROWS), F32), V((8, 4, 1, UROWS), F32), V((2, SEL, BLK, UROWS), BF16),
        V((NZ, 128, DI), BF16), V((DI, NZ * 128), BF16), V((NZ, 16, 8), BF16), V((NZ, 128, 128), F32),
        V((SEL, BLK, DI), BF16), V((SPAN // 128, 8, 128), I32),
        V((4, 16, SPAN), F32), V((4, 16, SPAN), BF16), V((2, 16, SPAN), BF16), V((2, 16, SPAN), BF16),
        V((NZ * 128, SPAN), BF16), V((NZ, 128, 128), F32), V((SEL, BLK, DI), F32),
        V((SEL, 32, DI), BF16), V((SEL, 32, DI), BF16),
        V((4, SEL * 8, DI), BF16), V((4, SEL * 8, DI), BF16), V((2, SEL + 1, 8, DI), F32),
        V((NCTX, 32, DI), BF16), V((NCTX, 32, DI), BF16),
        V((NZ, 144, DI), BF16), V((8, 144, DI), BF16), V((8, 128), F32), V((8, 128), F32),
        dma((2,)), dma((NCTX,)), dma((NCTX,)), dma((1,)),
        dma((4,)), dma((4,)), dma((8,)), dma((8,)), dma((8,)), dma((8,)),
        dma((NCOL,)), dma((NCOL,)), dma((NCOL,)), dma((NCOL,)),
        dma((2,)), dma((2,)), dma((1,)), dma((1,)), dma((1,)), dma((1,)),
        dma((4,)), dma((4,)), dma((NCTX,)), dma((NCTX,)), dma((8,)), dma((8,)), dma((1,)), dma((1,)),
    ]
    gk, gq, gw, kl = pl.pallas_call(
        kernel,
        out_shape=[
            jax.ShapeDtypeStruct((BLK * 8, DI), F32),
            jax.ShapeDtypeStruct((128 * 8, DI), F32),
            jax.ShapeDtypeStruct((128, 8), F32),
            jax.ShapeDtypeStruct((1, 128), F32),
        ],
        in_specs=[vmem, hbm, hbm, hbm, hbm, vmem],
        out_specs=[vmem] * 4,
        scratch_shapes=scratch,
        compiler_params=pltpu.CompilerParams(
            collective_id=0, has_side_effects=True, vmem_limit_bytes=62 * 1024 * 1024
        ),
        name="indexer_step",
    )(
        sel_blocks,
        latents.reshape(BLK, BLK, LAT),
        idx_keys.reshape(BLK, BLK, DI),
        mla_query,
        idx_query.reshape(128 * 8, DI),
        idx_weight,
    )
    return kl[0, 0:16], gq.reshape(128, 8, DI), gw, gk.reshape(BLK, 8, DI)


def solution(mesh):
    in_specs = (
        P("ctx", None),
        P("ctx", None),
        P("ctx", "head", None),
        P("ctx", "head", None),
        P("ctx", "head"),
        P("ctx", None),
    )
    out_specs = (
        P(("ctx", "head")),
        P("ctx", "head", None),
        P("ctx", "head"),
        P("ctx", "head", None),
    )
    return jax.shard_map(local, mesh=mesh, in_specs=in_specs, out_specs=out_specs, check_vma=False)
```

time: 521 us -> 134 us (0.26)
  the two profiles are of different devices: /device:TPU:2 before, /device:TPU:1 now
where the time goes in v1:
time: 134 us; the launch traced here: 133 us
  Pallas kernels  112 us (84%)
  local copies, waits for them, and re-layouts  20.2 us (15%)
    pallas_call x1, Pallas kernels, local(): pl.pallas_call(kernel, out_shape=[jax.ShapeDtypeStruct((BLK * 8, DI), F32...  112 us
    unnamed x6, local copies, waits for them, and re-layouts  19 us

profile of v1, /device:TPU:1, one launch (start us, length us, event | category | flops | bytes accessed | tf_op | source)
XLA Modules:
  0.0 133.1 jit_solution(4358466135719307052)
XLA Ops:
  0.6 1.4 %copy.12.iw_in = bf16[128,8]{1,0:T(8,128)(2,1)} copy(bf16[128,8]{0,1:T(8,128)(2,1)} %param.10) | data formatting | bytes 4096 | tf_op args[4]
  2.0 4.9 %copy.11.mq_hbm = bf16[128,16,576]{2,1,0:T(8,128)(2,1)} copy(bf16[128,16,576]{0,2,1:T(8,128)(2,1)} %param.8) | data formatting | bytes 4718592 | tf_op args[2]
  6.9 7.7 %copy.10 = bf16[4096,576]{1,0:T(8,128)(2,1)} copy(bf16[4096,576]{0,1:T(8,128)(2,1)} %param.6) | data formatting | bytes 9437184 | tf_op args[0]
  14.6 112.3 %indexer_step.1 = (f32[512,128]{1,0:T(8,128)}, f32[1024,128]{1,0:T(8,128)}, f32[128,8]{1,0:T(8,128)}, f32[1,128]{1,0:T(1,128)}) custom-call(s32[2,32]{1,0:T(2,128)} %sel_in.1, bf16[64,64,576]{2,1,0:T(8,128)(2,1)} %bitcast.7, bf16[64,64,128]{2,1,0:T(8,128)(2,1)} %bitcast.8, bf16[128,16,576]{2,1,0:T(8,128)(2,1)} %copy.11.mq_hbm, bf16[1024,128]{1,0:T(8,128)(2,1)} %bitcast.10, ...), custom_call_target="tpu_custom_call" | custom-call | tf_op jit(solution)/shard_map/indexer_step/pallas_call | solution.py:623
  126.9 1.2 slice_bitcast_fusion
  128.0 1.5 %copy.13 = f32[128,8]{0,1:T(8,128)} copy(f32[128,8]{1,0:T(8,128)} %get-tuple-element.14) | data formatting | bytes 8192
  129.5 1.9 %copy.16 = f32[128,8,128]{2,1,0:T(8,128)} copy(f32[128,8,128]{2,1,0:T(8,128)} %bitcast.9) | data formatting | bytes 1048576
  131.4 1.7 %copy.17 = f32[64,8,128]{2,1,0:T(8,128)} copy(f32[64,8,128]{2,1,0:T(8,128)} %bitcast.11) | data formatting | bytes 524288

commit v2 on v1

v2 whole, which is shorter than its diff:
```python
import functools
import math

import jax
import jax.numpy as jnp
from jax import lax
from jax.experimental import pallas as pl
from jax.experimental.pallas import tpu as pltpu
from jax.sharding import PartitionSpec as P

MESH = pl.DeviceIdType.MESH
LAT, DI, BLK, SEL = 576, 128, 64, 32
HEADS = 128
NZ, SIDE = 8, 4
NCOL = SIDE * SIDE
NCTX = 2 * NCOL
CONTEXT, QUERIES = 131072, 4096
SPAN = SEL * BLK
EXT = 640
WIDE = EXT + DI
FLOOR = -1e30
LOW = -2e30
EXP_SCALE = 192.0**-0.5 * math.log2(math.e)
IDX_SCALE = DI**-0.5
UROWS = 512
F32, BF16, I32 = jnp.float32, jnp.bfloat16, jnp.int32

OFFSETS = [(0, 0)] + sorted(
    [(i // SIDE, i % SIDE) for i in range(1, NCOL)], key=lambda o: -((o[0] == 2) + (o[1] == 2))
)
CODES = [dy * SIDE + dx for dy, dx in OFFSETS]


def pick(index, values):
    out = values[0]
    for i in range(1, len(values)):
        out = jnp.where(index == i, values[i], out)
    return out


def nt(a, b):
    return lax.dot_general(a, b, (((1,), (1,)), ((), ())), preferred_element_type=F32)


def kernel(
    sel_in, lat_hbm, ik_hbm, mq_hbm, iq_hbm, iw_in,
    gk_out, gq_out, kl_out,
    lat, ikv, selall, tbl, tbs, tbl1, tbs1, stage, rs, held, kbuf, qt, qbuf, qx, prob, mrun, zrun, mchunk, wts, xbuf, xs,
    iq, iqt, iwf, iw, wcol, ikc, kpos, tq, tqb, tsib, tfar, gwacc, gkf, gsend, grecv, kz, kr, kc,
    pm, pr, gqm, gqr, klm, klr,
    ld_s, lq_s, li_s, sel_s, sel_r, tb_s, q_s, q_r, iq_s, iq_r, iw_s, iw_r, st_s, st_r, fw_s, fw_r,
    ts_s, ts_r, tf_s, tf_r, gs_s, gs_r, kz_s, kz_r, pm_s, pm_r, gq_s, gq_r, kl_s, kl_r,
):
    me = lax.axis_index("ctx")
    z = lax.axis_index("head")
    k, core = me // 2, me % 2
    ky, kx = k // SIDE, k % SIDE
    sib = 2 * k + 1 - core
    rho = z % 4
    half = z // 4
    src_ctx = 2 * k + rho // 2
    blk_b = rho % 2
    t_own = 2 * half + core

    def column(code, sign, c):
        dy, dx = code // SIDE, code % SIDE
        sign = sign * (1 - 2 * c)
        return ((ky + sign * dy + SIDE) % SIDE) * SIDE + (kx + sign * dx + SIDE) % SIDE

    def send(src, dst, ssem, rsem, ctx, head):
        own = jnp.logical_and(ctx == me, head == z)
        remote = pltpu.make_async_remote_copy(
            src, dst, ssem, rsem, device_id={"ctx": ctx, "head": head}, device_id_type=MESH
        )

        @pl.when(own)
        def _():
            pltpu.make_async_copy(src, dst, rsem).start()

        @pl.when(jnp.logical_not(own))
        def _():
            remote.start()

        def finish():
            @pl.when(jnp.logical_not(own))
            def _():
                remote.wait_send()

        return finish

    def send_parts(src, dst, ssem, rsem, ctx, head, early):
        own = jnp.logical_and(ctx == me, head == z)
        away = jnp.logical_not(own)
        copy = remote(src, dst, ssem, rsem, ctx, head)

        def first():
            @pl.when(own)
            def _():
                pltpu.make_async_copy(src, dst, rsem).start()

            @pl.when(jnp.logical_and(away, early))
            def _():
                copy.start()

        def second():
            @pl.when(jnp.logical_and(away, jnp.logical_not(early)))
            def _():
                copy.start()

        def done():
            @pl.when(away)
            def _():
                copy.wait_send()

        return first, second, done

    def remote(src, dst, ssem, rsem, ctx, head):
        return pltpu.make_async_remote_copy(
            src, dst, ssem, rsem, device_id={"ctx": ctx, "head": head}, device_id_type=MESH
        )

    def arrived(dst, rsem):
        pltpu.make_async_copy(dst, dst, rsem).wait()

    pending = []

    def load_query(h):
        return pltpu.make_async_copy(
            mq_hbm.at[h],
            xbuf.at[h // 8, pl.ds(9 * (h // 4 % 2), 9), :, pl.ds(pl.multiple_of(h % 4 * 128, 128), 128)],
            lq_s.at[h],
        )

    def load_latents(n):
        return pltpu.make_async_copy(
            lat_hbm.at[:, :, pl.ds(pl.multiple_of(n * 128, 128), 128)], lat.at[n], ld_s.at[n]
        )

    load_ik = pltpu.make_async_copy(ik_hbm, ikv, li_s.at[0])
    for h in range(16):
        load_query(h).start()

    def start_latents(n, carry):
        load_latents(n).start()
        return carry

    lax.fori_loop(0, BLK // 2, start_latents, 0)
    load_ik.start()
    barrier = pltpu.get_barrier_semaphore()

    def greet_plane(d, carry):
        pl.semaphore_signal(
            barrier, inc=1, device_id={"ctx": (me + d) % NCTX, "head": z}, device_id_type=MESH
        )
        return carry

    def greet_column(d, carry):
        for c in range(2):
            pl.semaphore_signal(
                barrier, inc=1, device_id={"ctx": 2 * k + c, "head": (z + d) % NZ}, device_id_type=MESH
            )
        return carry

    lax.fori_loop(1, NCTX, greet_plane, 0)
    lax.fori_loop(1, NZ, greet_column, 0)
    selall[pl.ds(me, 1), 0:2, 0:SEL] = sel_in[...].reshape(1, 2, SEL)
    iwf[...] = iw_in[...].astype(F32)

    def turn_query(h, carry):
        tails = []
        for e in range(2):
            hh = h + 8 * e
            load_query(hh).wait()
            raw = xbuf.at[e, pl.ds(9 * (h // 4), 9), :, pl.ds(pl.multiple_of(h % 4 * 128, 128), 128)][...]
            rows = raw[0:8].reshape(512, 128).T
            for n in range(4):
                for t in range(4):
                    qt[n, pl.ds(16 * t + hh, 1)] = rows[32 * n : 32 * n + 32, 128 * t : 128 * t + 128].reshape(
                        1, 32, 128
                    )
            tails.append(raw[8])
        tail = jnp.concatenate(tails, axis=0).T
        for n in range(4):
            qt[n, pl.ds(64 + h, 1)] = tail[32 * n : 32 * n + 32, :].reshape(1, 32, 128)
        return carry

    lax.fori_loop(0, 8, turn_query, 0)
    pl.semaphore_wait(barrier, NCTX - 1 + 2 * (NZ - 1))

    def sel_copy(d):
        return remote(
            selall.at[me], selall.at[me], sel_s.at[d], sel_r.at[me], (me + d) % NCTX, z
        )

    def sel_start(d, carry):
        sel_copy(d).start()
        return carry

    lax.fori_loop(1, NCTX, sel_start, 0)

    far_sends = []
    for b in range(2):
        r = 2 * core + b
        d = (r - z + 8) % 4
        for hq in range(2):
            dz = pick(d, [0, 1, 2, 7] if hq == 0 else [0, 1, 6, 7])
            tcore = pick(d, [0, 0, 0, 1] if hq == 0 else [1, 0, 1, 1])
            unit = pick(d, [0, 1, 3, 1] if hq == 0 else [0, 2, 3, 2])
            first, second, done = send_parts(
                qt.at[2 * b + hq], qbuf.at[unit],
                q_s.at[2 * b + hq], q_r.at[unit], 2 * k + tcore, (z + dz) % NZ, d != 2,
            )
            first()
            far_sends.append(second)
            pending.append(done)
    for second in far_sends:
        second()

    def sel_wait(d, carry):
        src = (me + d) % NCTX
        arrived(selall.at[src], sel_r.at[src])
        return carry

    lax.fori_loop(1, NCTX, sel_wait, 0)
    lane = lax.broadcasted_iota(I32, (NCTX, 128), 1)
    sub = lax.broadcasted_iota(I32, (NCTX, 128), 0)
    lane_f = lane.astype(F32)
    sub3 = lax.broadcasted_iota(I32, (NCTX, 8, 128), 1)

    def rows_of(b):
        return jnp.sum(jnp.where(sub3 == b, selall[...], 0).astype(F32), axis=1).astype(I32)

    def two(match, values):
        first = jnp.min(jnp.where(match, lane_f, 128.0), axis=1, keepdims=True)
        hit0 = jnp.logical_and(match, lane_f == first)
        hit1 = jnp.logical_and(match, lane_f > first)
        v0 = jnp.sum(jnp.where(hit0, values, 0.0), axis=1, keepdims=True)
        v1 = jnp.sum(jnp.where(hit1, values, 0.0), axis=1, keepdims=True)
        return v0, v1

    def lanes(columns):
        out = jnp.zeros((NCTX, 128), F32)
        for i, c in enumerate(columns):
            out = jnp.where(lane == i, c, out)
        return out

    listed = lane < SEL
    wanted = []
    for b in range(2):
        rows = rows_of(b)
        match = jnp.logical_and(listed, rows // BLK == me)
        v0, v1 = two(match, (rows % BLK + 1).astype(F32))
        wanted += [v0 - 1.0, v1 - 1.0]
    table1 = lanes(wanted)
    tbl1[...] = table1.astype(I32)
    to_smem1 = pltpu.make_async_copy(tbl1, tbs1, tb_s.at[1])
    to_smem1.start()

    to_smem1.wait()
    load_ik.wait()

    def wait_latents(n, carry):
        load_latents(n).wait()
        return carry

    lax.fori_loop(0, BLK // 2, wait_latents, 0)

    lane_b = lax.broadcasted_iota(I32, (BLK, 128), 1)

    def gather(code, into):
        ctx = 2 * column(code, 1, core) + rho // 2
        tails, odds = [], []
        for r in range(2):
            index = jnp.clip(tbs1[ctx, 2 * blk_b + r], 0, BLK - 1)
            odd = index % 2 == 1
            raw = lat[pl.ds(index // 2, 1)].reshape(9, BLK, 128)
            rows = raw[0:8].reshape(512, 128).T
            rows = jnp.where(odd, rows[BLK:, :], rows[:BLK, :])
            for t in range(4):
                into[4 * r + t] = rows[:, 128 * t : 128 * t + 128]
            tails.append(raw[8])
            odds.append(odd)
            into[9 + r] = ikv[pl.ds(index, 1)].reshape(BLK, DI)
        tail = jnp.concatenate(tails, axis=0).T.astype(F32)
        tails = [jnp.where(odd, tail[BLK:, :], tail[:BLK, :]) for odd in odds]
        into[8] = jnp.where(lane_b < BLK, tails[0], tails[1]).astype(BF16)

    def stage_copy(i):
        to = 2 * column(pick(i, CODES), 1, core) + core
        return remote(stage.at[i], rs.at[i, core], st_s.at[i], st_r.at[i], to, z)

    def stage_send(i, carry):
        gather(pick(i, CODES), stage.at[i])
        stage_copy(i).start()
        return carry

    lax.fori_loop(1, NCOL, stage_send, 0)
    for b in range(2):
        for t in range(4):
            tz = 2 * core + b + 4 * (t // 2)
            tc = 2 * k + t % 2
            pending.append(
                send(
                    iq_hbm.at[pl.ds((BLK * b + 16 * t) * 8, 128)], iq.at[z],
                    iq_s.at[4 * b + t], iq_r.at[z], tc, tz,
                )
            )
            pending.append(
                send(iwf, iw.at[z], iw_s.at[4 * b + t], iw_r.at[z], tc, tz)
            )
    gather(0, rs.at[0, core])

    sub8 = lax.broadcasted_iota(I32, (8, 128), 0)

    def row_of(ctx, b):
        tile = selall[pl.ds(ctx, 1)].reshape(8, 128)
        return jnp.sum(jnp.where(sub8 == b, tile, 0).astype(F32), axis=0, keepdims=True)

    def by_owner(row):
        row = jnp.broadcast_to(row.astype(I32), (NCTX, 128))
        match = jnp.logical_and(listed, row // BLK == sub)
        return two(match, row.astype(F32) + 1.0)

    def use_order(col_index, odd):
        dy = ky - col_index // SIDE
        dx = kx - col_index % SIDE
        dy, dx = jnp.where(odd, -dy, dy), jnp.where(odd, -dx, dx)
        code = ((dy + SIDE) % SIDE) * SIDE + (dx + SIDE) % SIDE
        place = jnp.zeros_like(code)
        for i, c in enumerate(CODES):
            place = jnp.where(code == c, i, place)
        return place * 2 + odd.astype(I32)

    order = use_order(sub // 2, sub % 2 == 1)
    order_lane = use_order(lane % NCTX // 2, lane % 2 == 1)
    before = jnp.where(jnp.logical_and(order_lane < order, lane < NCTX), 1.0, 0.0)[:, 0:NCTX].astype(BF16)

    def number(row):
        v0, v1 = by_owner(row)
        has0, has1 = v0 > 0.5, v1 > 0.5
        count = jnp.where(has0, 1.0, 0.0) + jnp.where(has1, 1.0, 0.0)
        count = jnp.broadcast_to(count, (NCTX, 128)).astype(BF16)
        n0 = jnp.dot(before, count, preferred_element_type=F32)
        return v0, v1, jnp.where(has0, n0, float(SEL)), jnp.where(has1, n0 + 1.0, float(SEL))

    v0, v1, n0, n1 = number(row_of(src_ctx, blk_b))
    hit0 = jnp.logical_and(lane_f == n0, listed)
    hit1 = jnp.logical_and(lane_f == n1, listed)
    slot = order.astype(F32) * 2.0

    def along(a, b):
        total = jnp.where(hit0, a, 0.0) + jnp.where(hit1, b, 0.0)
        return jnp.sum(total, axis=0, keepdims=True)

    slots = along(slot, slot + 1.0)
    blocks = along(v0 - 1.0, v1 - 1.0)
    columns = [v0, v1]
    for b in range(2):
        _, _, m0, m1 = number(row_of(me, b))
        columns += [m0, m1]
    tbl[0:NCTX, :] = lanes(columns).astype(I32)
    tbl[NCTX : NCTX + 8, :] = jnp.where(
        sub8 == 0, jnp.broadcast_to(slots, (8, 128)), jnp.broadcast_to(blocks, (8, 128))
    ).astype(I32)
    to_smem = pltpu.make_async_copy(tbl, tbs, tb_s.at[0])
    to_smem.start()
    to_smem.wait()

    def forward_copy(i):
        return remote(rs.at[i, core], rs.at[i, core], fw_s.at[i], fw_r.at[i], sib, z)

    key_off = lax.broadcasted_iota(I32, (BLK, 128), 0)
    q_base = CONTEXT - QUERIES + src_ctx * 128 + blk_b * BLK
    reach = lane_b - BLK + q_base - key_off

    def forward(c):
        for e in range(2):
            i = 2 * c + e

            @pl.when(i > 0)
            def _():
                arrived(rs.at[i, core], st_r.at[i])

            forward_copy(i).start()

    def settle(c):
        for e in range(2):
            i = 2 * c + e
            arrived(rs.at[i, 1 - core], fw_r.at[i])
            held[pl.ds(i, 1)] = rs[pl.ds(i, 1)]

    def collect(g):
        def block(j, carry):
            n = 8 * g + j
            s = jnp.clip(tbs[NCTX, n], 0, 63)
            odd = s % 2 == 1
            place = held.at[pl.ds(s // 4, 1), pl.ds(s // 2 % 2, 1)]
            at = pl.ds(pl.multiple_of(j * BLK, BLK), BLK)
            for t in range(4):
                kbuf[g, at, 128 * t : 128 * t + 128] = place[:, :, pl.ds(s % 2 * 4 + t, 1)].reshape(BLK, 128)
            tail = place[:, :, 8].reshape(BLK, 128).astype(F32)
            tail = jnp.where(odd, pltpu.roll(tail, 64, 1), tail)
            bias = jnp.where(tbs[NCTX + 1, n] * BLK > reach, FLOOR, 0.0)
            kbuf[g, at, 512:EXT] = jnp.where(lane_b < BLK, tail, bias).astype(BF16)
            ikc[pl.ds(n, 1)] = place[:, :, pl.ds(9 + s % 2, 1)].reshape(1, BLK, DI)
            return carry

        lax.fori_loop(0, 8, block, 0)

    def query_unit(u):
        arrived(qbuf.at[u], q_r.at[u])
        first_q = pick(u, [32 * core, 0, 32, 32 * core])
        row = lax.broadcasted_iota(I32, (256, 128), 0) % 32 + first_q
        col = lax.broadcasted_iota(I32, (256, 128), 1)
        hot = jnp.where(row == col - BLK, 1.0, 0.0)
        for t in range(4):
            qx[u, :, 128 * t : 128 * t + 128] = qbuf[u, 16 * t : 16 * t + 16].reshape(UROWS, 128)
        tail = qbuf[u, 64:72].reshape(256, 128).astype(F32)
        qx[u, 0:256, 512:EXT] = jnp.where(col < BLK, tail, hot).astype(BF16)
        qx[u, 256:512, 512:EXT] = jnp.where(col < BLK, pltpu.roll(tail, 64, 1), hot).astype(BF16)
        mrun[u] = jnp.full((1, UROWS), LOW, F32)
        zrun[u] = jnp.zeros((1, UROWS), F32)

    def pair(u, c):
        keys = kbuf[c]
        parts = [nt(keys, qx[u, 256 * h : 256 * h + 256, :]) for h in range(2)]
        for h in range(2):
            s = parts[h]
            lanes_h = slice(256 * h, 256 * h + 256)
            old = mrun[u, :, lanes_h]
            new = jnp.maximum(old, jnp.max(s, axis=0, keepdims=True))
            p = jnp.exp2((s - new) * EXP_SCALE)
            zrun[u, :, lanes_h] = zrun[u, :, lanes_h] * jnp.exp2((old - new) * EXP_SCALE) + jnp.sum(
                p, axis=0, keepdims=True
            )
            mrun[u, :, lanes_h] = new
            mchunk[c, u, :, lanes_h] = new
            prob[c, pl.ds(8 * u, 8), :, lanes_h] = p.astype(BF16).reshape(8, BLK, 256)

    def group(g):
        collect(g)

        def step(u, carry):
            pair(u, g)
            return carry

        lax.fori_loop(0, 4, step, 0)

    def step(c, carry):
        forward(c)

        @pl.when(c > 0)
        def _():
            settle(c - 1)

        return carry

    lax.fori_loop(0, 6, step, 0)
    for u in range(4):
        query_unit(u)
    group(0)
    step(6, 0)
    group(1)
    own_q = lax.broadcasted_iota(I32, (128, 128), 0) // 8 + BLK * blk_b + 16 * t_own
    own_q = own_q == lax.broadcasted_iota(I32, (128, 128), 1)
    for s in range(NZ):
        arrived(iq.at[s], iq_r.at[s])
        arrived(iw.at[s], iw_r.at[s])
        w = jnp.broadcast_to(iw[s].reshape(1, 8, 128), (16, 8, 128)).reshape(128, 128)
        w = jnp.sum(jnp.where(own_q, w, 0.0), axis=1, keepdims=True)
        wcol[s] = jnp.broadcast_to(w * IDX_SCALE, (128, 128))
        iqt[:, 128 * s : 128 * (s + 1)] = iq[s].astype(F32).T.astype(BF16)

    step(7, 0)
    group(2)
    settle(7)
    group(3)

    for u in range(4):
        scale = 1.0 / (zrun[u] * HEADS)
        for c in range(4):
            w = jnp.exp2((mchunk[c, u] - mrun[u]) * EXP_SCALE) * scale
            wts[c, u] = jnp.broadcast_to(w, (16, UROWS)).astype(BF16)

    def compact(i, carry):
        c, j = i // 8, i % 8

        def part(u):
            p = prob[pl.ds(c, 1), pl.ds(8 * u + j, 1)].reshape(4, 16, UROWS)
            return p * wts[pl.ds(c, 1), pl.ds(u, 1)].reshape(1, 16, UROWS)

        def narrow(p):
            p = p.reshape(BLK, UROWS).astype(F32)
            p = (p[:, 0:128] + p[:, 128:256]) + (p[:, 256:384] + p[:, 384:512])
            return p.astype(BF16).reshape(1, BLK, 128)

        xs[0, pl.ds(i, 1)] = narrow(part(0) + part(3) + part(1 + core))
        xs[1, pl.ds(i, 1)] = narrow(part(2 - core))
        return carry

    lax.fori_loop(0, SEL, compact, 0)
    fold = jnp.where(
        lax.broadcasted_iota(I32, (32, 128), 0) == lax.broadcasted_iota(I32, (32, 128), 1) % 32, 1.0, 0.0
    ).astype(BF16)
    for x in range(2):
        part = nt(fold, xs[x].reshape(SPAN, 128))
        h = core if x == 0 else 1 - core
        tq[pl.ds(2 * h, 2)] = part.reshape(2, 16, SPAN)
        tqb[pl.ds(2 * h, 2)] = part.astype(BF16).reshape(2, 16, SPAN)
    sib_copies = [
        remote(tqb.at[1 - core + 2 * h], tsib.at[h], ts_s.at[h], ts_r.at[h], sib, z) for h in range(2)
    ]
    for copy in sib_copies:
        copy.start()

    TILE = 512

    def dots_of(s, kt):
        keys = ikc[pl.ds(kt * (TILE // BLK), TILE // BLK)].reshape(TILE, DI)
        return nt(iq[s], keys)

    def logit_tile(kt):
        acc = jnp.zeros((128, TILE), F32)
        for s in range(NZ):
            w = jnp.concatenate([wcol[s]] * (TILE // 128), axis=1)
            acc = acc + w * jnp.maximum(dots_of(s, kt), 0.0)
        return jnp.sum(acc.reshape(16, 8, TILE), axis=1)

    logit_tiles = [logit_tile(0)]

    def positions(i, carry):
        l8 = lax.broadcasted_iota(I32, (8, 128), 1)
        a, b = tbs[NCTX + 1, 2 * i] * BLK, tbs[NCTX + 1, 2 * i + 1] * BLK
        kpos[pl.ds(i, 1)] = (jnp.where(l8 < BLK, a, b) + l8 % BLK).reshape(1, 8, 128)
        return carry

    lax.fori_loop(0, SPAN // 128, positions, 0)
    q_pos = q_base + 16 * t_own + lax.broadcasted_iota(I32, (16, 128), 0)
    visible = jnp.concatenate(
        [jnp.concatenate([kpos[i]] * 2, axis=0) <= q_pos for i in range(SPAN // 128)], axis=1
    )

    for h, copy in enumerate(sib_copies):
        arrived(tsib.at[h], ts_r.at[h])
        copy.wait_send()
    far = 1 - half
    mine = tq[pl.ds(2 * half + core, 1)].reshape(16, SPAN) + tsib[pl.ds(half, 1)].reshape(16, SPAN).astype(F32)
    other = tq[pl.ds(2 * far + core, 1)].reshape(16, SPAN) + tsib[pl.ds(far, 1)].reshape(16, SPAN).astype(F32)
    tfar[0] = other.astype(BF16)
    far_copy = remote(tfar.at[0], tfar.at[1], tf_s.at[0], tf_r.at[0], me, (z + 4) % NZ)
    far_copy.start()
    logit_tiles += [logit_tile(kt) for kt in range(1, SPAN // TILE)]
    logits = jnp.concatenate(logit_tiles, axis=1)
    masked = jnp.where(visible, logits, FLOOR)
    shifted = masked - jnp.max(masked, axis=1, keepdims=True)
    log_norm = jnp.log(jnp.sum(jnp.exp(shifted), axis=1, keepdims=True))
    log_ratio = shifted - log_norm
    predicted = jnp.where(visible, jnp.exp(log_ratio), 0.0)
    arrived(tfar.at[1], tf_r.at[0])
    target = mine + tfar[1].astype(F32)
    positive = target > 0.0
    entropy = jnp.sum(
        jnp.where(positive, target * jnp.log(jnp.where(positive, target, 1.0)), 0.0), axis=1, keepdims=True
    )
    cross = jnp.sum(jnp.where(visible, target * log_ratio, 0.0), axis=1, keepdims=True)
    gradient = jnp.where(visible, SPAN * (predicted - target), 0.0).astype(BF16).astype(F32)
    divergence = entropy - cross
    spot = lax.broadcasted_iota(I32, (16, 128), 0) == lax.broadcasted_iota(I32, (16, 128), 1)
    klm[...] = jnp.broadcast_to(
        jnp.sum(jnp.where(spot, divergence, 0.0), axis=0, keepdims=True), (8, 128)
    )
    pending.append(
        send(klm, klr, kl_s.at[0], kl_r.at[0], src_ctx, 4 * blk_b + t_own)
    )

    KB = TILE // BLK

    def swap(kt):
        part = pl.ds(kt * KB, KB)
        return remote(gsend.at[part], grecv.at[part], gs_s.at[kt], gs_r.at[kt], sib, z)

    def cores_sum(kt):
        here = slice(kt * KB, (kt + 1) * KB)
        arrived(grecv.at[pl.ds(kt * KB, KB)], gs_r.at[kt])
        both = gkf[here, pl.ds(32 * core, 32), :] + grecv[here].astype(F32)
        to = 2 * blk_b + half
        for t in range(4):
            kz[t, kt] = both[:, 8 * t : 8 * t + 8, :].reshape(KB * 8, DI).astype(BF16)
            pending.append(
                send(
                    kz.at[t, kt], kr.at[to, kt], kz_s.at[4 * t + kt], kz_r.at[4 * to + kt],
                    src_ctx, 4 * core + t,
                )
            )

    for kt in range(SPAN // TILE):
        g = gradient[:, kt * TILE : (kt + 1) * TILE]
        g = jnp.broadcast_to(g.reshape(16, 1, TILE), (16, 8, TILE)).reshape(128, TILE)
        for s in range(NZ):
            dots = dots_of(s, kt)
            weighted = g * jnp.maximum(dots, 0.0)
            lanesum = weighted[:, 0:128]
            for i in range(1, TILE // 128):
                lanesum = lanesum + weighted[:, 128 * i : 128 * (i + 1)]
            gwacc[s] = lanesum if kt == 0 else gwacc[s] + lanesum
            w = jnp.concatenate([wcol[s]] * (TILE // 128), axis=1)
            prob[kt, 2 * s : 2 * s + 2] = (
                jnp.where(dots > 0.0, g * w, 0.0).astype(BF16).reshape(2, BLK, TILE)
            )
        part = jnp.dot(iqt[...], prob[kt, 0 : 2 * NZ].reshape(NZ * 128, TILE), preferred_element_type=F32)
        here = slice(kt * KB, (kt + 1) * KB)
        gkf[here] = part.T.reshape(KB, BLK, DI)
        gsend[here] = gkf[here, pl.ds(32 * (1 - core), 32), :].astype(BF16)
        swap(kt).start()
        if kt > 0:
            cores_sum(kt - 1)
    unspread = jnp.where(
        lax.broadcasted_iota(I32, (16, 128), 0) == lax.broadcasted_iota(I32, (16, 128), 1) // 8, 1.0, 0.0
    )
    diag_j = lax.broadcasted_iota(I32, (128, 128), 0) % 8 == lax.broadcasted_iota(I32, (128, 128), 1)
    for s in range(NZ):
        gq = jnp.dot(
            jnp.concatenate(
                [prob[kt, 2 * s : 2 * s + 2].reshape(128, TILE) for kt in range(SPAN // TILE)], axis=1
            ),
            ikc[...].reshape(SPAN, DI), preferred_element_type=F32
        )
        gqm[s, 0:128, :] = gq.astype(BF16)
        gw = jnp.sum(gwacc[s], axis=1, keepdims=True) * IDX_SCALE
        gw = jnp.dot(
            unspread, jnp.where(diag_j, gw, 0.0), preferred_element_type=F32, precision=lax.Precision.HIGHEST
        )
        gqm[s, 128:144, :] = gw.astype(BF16)
    cores_sum(SPAN // TILE - 1)
    for s in range(NZ):
        pending.append(
            send(
                gqm.at[s], gqr.at[4 * blk_b + t_own], gq_s.at[s], gq_r.at[4 * blk_b + t_own], src_ctx, s
            )
        )
    for kt in range(SPAN // TILE):
        swap(kt).wait_send()
    for b in range(2):
        for h in range(2):
            for kt in range(SPAN // TILE):
                arrived(kr.at[2 * b + h, kt], kz_r.at[4 * (2 * b + h) + kt])
        total = kr[2 * b].astype(F32) + kr[2 * b + 1].astype(F32)
        kc[b, 0:SEL] = total.reshape(SEL, 8, DI)
        kc[b, SEL : SEL + 1] = jnp.zeros((1, 8, DI), F32)

    def owner_copy(o):
        return remote(pm.at[o], pr.at[me], pm_s.at[o], pm_r.at[me], o, z)

    def owner_block(o):
        parts = []
        for b in range(2):
            for r in range(2):
                index = jnp.clip(tbs[o, 2 + 2 * b + r], 0, SEL)
                parts.append(kc[pl.ds(b, 1), pl.ds(index, 1)].reshape(8, DI))
        return jnp.concatenate(parts, axis=0).astype(BF16)

    def owner_of(i):
        return (me + i) % NCTX

    def owner_send(i, carry):
        o = owner_of(i)
        pm[pl.ds(o, 1)] = owner_block(o).reshape(1, 32, DI)
        owner_copy(o).start()
        return carry

    lax.fori_loop(1, NCTX, owner_send, 0)
    pr[pl.ds(me, 1)] = owner_block(me).reshape(1, 32, DI)

    col = lax.broadcasted_iota(I32, (128, 1024), 1)
    expand = jnp.where(col % 32 // 8 == lax.broadcasted_iota(I32, (128, 1024), 0), 1.0, 0.0).astype(BF16)
    wide = jnp.dot(table1.astype(BF16), expand, preferred_element_type=F32)
    col = lax.broadcasted_iota(I32, (NCTX, 1024), 1)
    wide = jnp.where(col // 32 == lax.broadcasted_iota(I32, (NCTX, 1024), 0), wide * 8.0, 0.0)
    code = jnp.sum(wide, axis=0, keepdims=True) + (
        lax.broadcasted_iota(I32, (1, 1024), 1) % 8
    ).astype(F32)
    row = lax.broadcasted_iota(I32, (512, 1024), 0).astype(F32)
    hot = jnp.where(row == code, 1.0, 0.0).astype(BF16)

    arrived(klr, kl_r.at[0])
    kl_out[...] = klr[...]
    for i in range(8):
        arrived(gqr.at[i], gq_r.at[i])
        gq_out[i] = gqr[i]

    def owner_wait(i, carry):
        o = owner_of(i)
        arrived(pr.at[o], pm_r.at[o])
        owner_copy(o).wait_send()
        return carry

    lax.fori_loop(1, NCTX, owner_wait, 0)
    gk_out[...] = jnp.dot(hot, pr[...].reshape(1024, DI), preferred_element_type=F32)

    for finish in pending:
        finish()
    far_copy.wait_send()

    def drain_sel(d, carry):
        sel_copy(d).wait_send()
        return carry

    def drain_stage(i, carry):
        stage_copy(i).wait_send()
        return carry

    lax.fori_loop(1, NCTX, drain_sel, 0)
    lax.fori_loop(1, NCOL, drain_stage, 0)

    def drain_forward(i, carry):
        forward_copy(i).wait_send()
        return carry

    lax.fori_loop(0, NCOL, drain_forward, 0)


def unpack(gk, gq, kl, gk_out, gq_out, gw_out, kl_out):
    gk_out[...] = gk[...].reshape(BLK, 8, DI)
    weights = []
    for i in range(8):
        gq_out[16 * i : 16 * (i + 1)] = gq[i, 0:128, :].astype(F32).reshape(16, 8, DI)
        weights.append(gq[i, 128:144, :].astype(F32))
    gw_out[...] = jnp.concatenate(weights, axis=0).T[0:8, :]
    kl_out[...] = kl[0, 0:16]


def local(latents, idx_keys, mla_query, idx_query, idx_weight, sel_blocks):
    V = pltpu.VMEM
    dma = pltpu.SemaphoreType.DMA
    hbm = pl.BlockSpec(memory_space=pl.ANY)
    vmem = pl.BlockSpec(memory_space=pltpu.VMEM)
    scratch = [
        V((BLK // 2, 9, BLK, 128), BF16), V((BLK, BLK, DI), BF16), V((NCTX, 8, 128), I32),
        V((NCTX + 8, 128), I32), pltpu.SMEM((NCTX + 8, 128), I32),
        V((NCTX, 128), I32), pltpu.SMEM((NCTX, 128), I32),
        V((NCOL, 11, BLK, 128), BF16), V((NCOL, 2, 11, BLK, 128), BF16),
        V((NCOL, 2, 11, BLK, 128), BF16), V((4, 512, EXT), BF16),
        V((4, 72, 32, 128), BF16), V((4, 72, 32, 128), BF16), V((4, UROWS, EXT), BF16),
        V((4, 32, BLK, UROWS), BF16), V((4, 1, UROWS), F32), V((4, 1, UROWS), F32),
        V((4, 4, 1, UROWS), F32), V((4, 4, 16, UROWS), BF16),
        V((2, SEL, BLK, UROWS), BF16), V((2, SEL, BLK, 128), BF16),
        V((NZ, 128, DI), BF16), V((DI, NZ * 128), BF16),
        V((8, 128), F32), V((NZ, 8, 128), F32), V((NZ, 128, 128), F32),
        V((SEL, BLK, DI), BF16), V((SPAN // 128, 8, 128), I32),
        V((4, 16, SPAN), F32), V((4, 16, SPAN), BF16), V((2, 16, SPAN), BF16), V((2, 16, SPAN), BF16),
        V((NZ, 128, 128), F32), V((SEL, BLK, DI), F32),
        V((SEL, 32, DI), BF16), V((SEL, 32, DI), BF16),
        V((4, 4, SEL * 2, DI), BF16), V((4, 4, SEL * 2, DI), BF16), V((2, SEL + 1, 8, DI), F32),
        V((NCTX, 32, DI), BF16), V((NCTX, 32, DI), BF16),
        V((NZ, 144, DI), BF16), V((8, 144, DI), BF16), V((8, 128), F32), V((8, 128), F32),
        dma((BLK // 2,)), dma((16,)), dma((1,)), dma((NCTX,)), dma((NCTX,)), dma((2,)),
        dma((4,)), dma((4,)), dma((8,)), dma((8,)), dma((8,)), dma((8,)),
        dma((NCOL,)), dma((NCOL,)), dma((NCOL,)), dma((NCOL,)),
        dma((2,)), dma((2,)), dma((1,)), dma((1,)), dma((4,)), dma((4,)),
        dma((16,)), dma((16,)), dma((NCTX,)), dma((NCTX,)), dma((8,)), dma((8,)), dma((1,)), dma((1,)),
    ]
    gk, gq, kl = pl.pallas_call(
        kernel,
        out_shape=[
            jax.ShapeDtypeStruct((BLK * 8, DI), F32),
            jax.ShapeDtypeStruct((8, 144, DI), BF16),
            jax.ShapeDtypeStruct((8, 128), F32),
        ],
        in_specs=[vmem, hbm, hbm, hbm, hbm, vmem],
        out_specs=[vmem] * 3,
        scratch_shapes=scratch,
        compiler_params=pltpu.CompilerParams(
            collective_id=0, has_side_effects=True, vmem_limit_bytes=62 * 1024 * 1024
        ),
        name="indexer_step",
    )(
        sel_blocks,
        latents.T.reshape(9, BLK, BLK * BLK),
        idx_keys.reshape(BLK, BLK, DI),
        mla_query.transpose(1, 2, 0).reshape(16, 9, BLK, 128),
        idx_query.reshape(128 * 8, DI),
        idx_weight.T,
    )
    grad_keys, grad_query, grad_weight, divergence = pl.pallas_call(
        unpack,
        out_shape=[
            jax.ShapeDtypeStruct((BLK, 8, DI), F32),
            jax.ShapeDtypeStruct((128, 8, DI), F32),
            jax.ShapeDtypeStruct((8, 128), F32),
            jax.ShapeDtypeStruct((16,), F32),
        ],
        in_specs=[vmem] * 3,
        out_specs=[vmem] * 4,
        name="unpack",
    )(gk, gq, kl)
    return divergence, grad_query, grad_weight.T, grad_keys


def solution(mesh):
    in_specs = (
        P("ctx", None),
        P("ctx", None),
        P("ctx", "head", None),
        P("ctx", "head", None),
        P("ctx", "head"),
        P("ctx", None),
    )
    out_specs = (
        P(("ctx", "head")),
        P("ctx", "head", None),
        P("ctx", "head"),
        P("ctx", "head", None),
    )
    return jax.shard_map(local, mesh=mesh, in_specs=in_specs, out_specs=out_specs, check_vma=False)
```

time: 134 us -> 106 us (0.79)
  local copies, waits for them, and re-layouts: 20.2 us -> 0 us
  Pallas kernels: 112 us -> 106 us
    unnamed x6 -> x0, local copies, waits for them, and re-layouts: 19 us -> none
    pallas_call x1, Pallas kernels: 112 us -> 104 us  [local(): pl.pallas_call(kernel, out_shape=[jax.ShapeDtypeStruct((BLK * 8, DI), F32...]
    pallas_call x0 -> x1, Pallas kernels: none -> 1.97 us  [local(): pl.pallas_call(unpack, out_shape=[jax.ShapeDtypeStruct((BLK, 8, DI), F32)...]
where the time goes in v2:
time: 106 us
  Pallas kernels  106 us (100%)
    pallas_call x1, Pallas kernels, local(): pl.pallas_call(kernel, out_shape=[jax.ShapeDtypeStruct((BLK * 8, DI), F32...  104 us

profile of v2, /device:TPU:1, one launch (start us, length us, event | category | flops | bytes accessed | tf_op | source)
XLA Modules:
  0.0 106.3 jit_solution(13666143004295525690)
XLA Ops:
  0.6 103.7 %indexer_step.1 = (f32[512,128]{1,0:T(8,128)}, bf16[8,144,128]{2,1,0:T(8,128)(2,1)}, f32[8,128]{1,0:T(8,128)}) custom-call(s32[2,32]{1,0:T(2,128)} %sel_in.1, bf16[9,64,4096]{2,1,0:T(8,128)(2,1)} %bitcast.10, bf16[64,64,128]{2,1,0:T(8,128)(2,1)} %bitcast.12, bf16[16,9,64,128]{3,2,1,0:T(8,128)(2,1)} %bitcast.11, bf16[1024,128]{1,0:T(8,128)(2,1)} %bitcast.13, ...), custom_call_target="tpu_custom_call" | custom-call | tf_op jit(solution)/shard_map/indexer_step/pallas_call | solution.py:762
  104.4 2.0 %unpack.1 = (f32[64,8,128]{2,1,0:T(8,128)}, f32[128,8,128]{2,1,0:T(8,128)}, f32[8,128]{1,0:T(8,128)}, f32[16]{0:T(128)}) custom-call(f32[512,128]{1,0:T(8,128)} %get-tuple-element.11.gk, bf16[8,144,128]{2,1,0:T(8,128)(2,1)} %get-tuple-element.12.gq, f32[8,128]{1,0:T(8,128)} %get-tuple-element.13.kl), custom_call_target="tpu_custom_call" | custom-call | tf_op jit(solution)/shard_map/unpack/pallas_call | solution.py:784

commit v3 on v2

--- a/solution.py
+++ b/solution.py
@@ -23,11 +23,11 @@
 EXP_SCALE = 192.0**-0.5 * math.log2(math.e)
 IDX_SCALE = DI**-0.5
 UROWS = 512
+IN_FLIGHT, LAG = 5, 6
 F32, BF16, I32 = jnp.float32, jnp.bfloat16, jnp.int32
 
-OFFSETS = [(0, 0)] + sorted(
-    [(i // SIDE, i % SIDE) for i in range(1, NCOL)], key=lambda o: -((o[0] == 2) + (o[1] == 2))
-)
+OFFSETS = [(0, 0), (0, 1), (0, 3), (1, 0), (3, 0), (1, 1), (3, 3), (1, 3), (3, 1)]
+OFFSETS += [(0, 2), (2, 0), (1, 2), (2, 1), (3, 2), (2, 3), (2, 2)]
 CODES = [dy * SIDE + dx for dy, dx in OFFSETS]
 
 
@@ -38,6 +38,10 @@
     return out
 
 
+def wrap(value, n):
+    return jnp.where(value >= n, value - n, value)
+
+
 def nt(a, b):
     return lax.dot_general(a, b, (((1,), (1,)), ((), ())), preferred_element_type=F32)
 
@@ -45,9 +49,9 @@
 def kernel(
     sel_in, lat_hbm, ik_hbm, mq_hbm, iq_hbm, iw_in,
     gk_out, gq_out, kl_out,
-    lat, ikv, selall, tbl, tbs, tbl1, tbs1, stage, rs, held, kbuf, qt, qbuf, qx, prob, mrun, zrun, mchunk, wts, xbuf, xs,
+    lat, ikv, selall, tbl, tbs, tbl1, tbs1, stage, rs, held, kbuf, qt, qbuf, qx, s_even, s_odd, prob, mrun, zrun, mchunk, wts, xbuf, xs,
     iq, iqt, iwf, iw, wcol, ikc, kpos, tq, tqb, tsib, tfar, gwacc, gkf, gsend, grecv, kz, kr, kc,
-    pm, pr, gqm, gqr, klm, klr,
+    pm, pr, gqm, gqr, klm, klr, lbuf, gbuf,
     ld_s, lq_s, li_s, sel_s, sel_r, tb_s, q_s, q_r, iq_s, iq_r, iw_s, iw_r, st_s, st_r, fw_s, fw_r,
     ts_s, ts_r, tf_s, tf_r, gs_s, gs_r, kz_s, kz_r, pm_s, pm_r, gq_s, gq_r, kl_s, kl_r,
 ):
@@ -65,28 +69,28 @@
     def column(code, sign, c):
         dy, dx = code // SIDE, code % SIDE
         sign = sign * (1 - 2 * c)
-        return ((ky + sign * dy + SIDE) % SIDE) * SIDE + (kx + sign * dx + SIDE) % SIDE
-
-    def send(src, dst, ssem, rsem, ctx, head):
-        own = jnp.logical_and(ctx == me, head == z)
-        remote = pltpu.make_async_remote_copy(
-            src, dst, ssem, rsem, device_id={"ctx": ctx, "head": head}, device_id_type=MESH
-        )
-
-        @pl.when(own)
-        def _():
-            pltpu.make_async_copy(src, dst, rsem).start()
-
-        @pl.when(jnp.logical_not(own))
-        def _():
-            remote.start()
-
-        def finish():
-            @pl.when(jnp.logical_not(own))
+        row = wrap(wrap(ky + sign * dy + SIDE, SIDE), SIDE)
+        return row * SIDE + wrap(wrap(kx + sign * dx + SIDE, SIDE), SIDE)
+
+    class send:
+        def __init__(self, src, dst, ssem, rsem, ctx, head):
+            self.own = jnp.logical_and(ctx == me, head == z)
+            self.here = (src, dst, rsem)
+            self.away = remote(src, dst, ssem, rsem, ctx, head)
+
+        def start(self):
+            @pl.when(self.own)
             def _():
-                remote.wait_send()
-
-        return finish
+                pltpu.make_async_copy(*self.here).start()
+
+            @pl.when(jnp.logical_not(self.own))
+            def _():
+                self.away.start()
+
+        def finish(self):
+            @pl.when(jnp.logical_not(self.own))
+            def _():
+                self.away.wait_send()
 
     def send_parts(src, dst, ssem, rsem, ctx, head, early):
         own = jnp.logical_and(ctx == me, head == z)
@@ -150,14 +154,14 @@
 
     def greet_plane(d, carry):
         pl.semaphore_signal(
-            barrier, inc=1, device_id={"ctx": (me + d) % NCTX, "head": z}, device_id_type=MESH
+            barrier, inc=1, device_id={"ctx": wrap(me + d, NCTX), "head": z}, device_id_type=MESH
         )
         return carry
 
     def greet_column(d, carry):
         for c in range(2):
             pl.semaphore_signal(
-                barrier, inc=1, device_id={"ctx": 2 * k + c, "head": (z + d) % NZ}, device_id_type=MESH
+                barrier, inc=1, device_id={"ctx": 2 * k + c, "head": wrap(z + d, NZ)}, device_id_type=MESH
             )
         return carry
 
@@ -189,7 +193,7 @@
 
     def sel_copy(d):
         return remote(
-            selall.at[me], selall.at[me], sel_s.at[d], sel_r.at[me], (me + d) % NCTX, z
+            selall.at[me], selall.at[me], sel_s.at[d], sel_r.at[me], wrap(me + d, NCTX), z
         )
 
     def sel_start(d, carry):
@@ -208,7 +212,7 @@
             unit = pick(d, [0, 1, 3, 1] if hq == 0 else [0, 2, 3, 2])
             first, second, done = send_parts(
                 qt.at[2 * b + hq], qbuf.at[unit],
-                q_s.at[2 * b + hq], q_r.at[unit], 2 * k + tcore, (z + dz) % NZ, d != 2,
+                q_s.at[2 * b + hq], q_r.at[unit], 2 * k + tcore, wrap(z + dz, NZ), d != 2,
             )
             first()
             far_sends.append(second)
@@ -217,7 +221,7 @@
         second()
 
     def sel_wait(d, carry):
-        src = (me + d) % NCTX
+        src = wrap(me + d, NCTX)
         arrived(selall.at[src], sel_r.at[src])
         return carry
 
@@ -289,26 +293,32 @@
         to = 2 * column(pick(i, CODES), 1, core) + core
         return remote(stage.at[i], rs.at[i, core], st_s.at[i], st_r.at[i], to, z)
 
-    def stage_send(i, carry):
+    def stage_send(n, carry):
+        i = n % NCOL
         gather(pick(i, CODES), stage.at[i])
-        stage_copy(i).start()
-        return carry
-
-    lax.fori_loop(1, NCOL, stage_send, 0)
+
+        @pl.when(i > 0)
+        def _():
+            stage_copy(i).start()
+
+        return carry
+
+    stage_send(NCOL, 0)
+    lax.fori_loop(1, IN_FLIGHT + 1, stage_send, 0)
     for b in range(2):
         for t in range(4):
             tz = 2 * core + b + 4 * (t // 2)
             tc = 2 * k + t % 2
-            pending.append(
+            for copy in (
                 send(
                     iq_hbm.at[pl.ds((BLK * b + 16 * t) * 8, 128)], iq.at[z],
                     iq_s.at[4 * b + t], iq_r.at[z], tc, tz,
-                )
-            )
-            pending.append(
-                send(iwf, iw.at[z], iw_s.at[4 * b + t], iw_r.at[z], tc, tz)
-            )
-    gather(0, rs.at[0, core])
+                ),
+                send(iwf, iw.at[z], iw_s.at[4 * b + t], iw_r.at[z], tc, tz),
+            ):
+                copy.start()
+                pending.append(copy.finish)
+    rs[0, pl.ds(core, 1)] = stage[0:1]
 
     sub8 = lax.broadcasted_iota(I32, (8, 128), 0)
 
@@ -373,21 +383,16 @@
     q_base = CONTEXT - QUERIES + src_ctx * 128 + blk_b * BLK
     reach = lane_b - BLK + q_base - key_off
 
-    def forward(c):
-        for e in range(2):
-            i = 2 * c + e
-
-            @pl.when(i > 0)
-            def _():
-                arrived(rs.at[i, core], st_r.at[i])
-
-            forward_copy(i).start()
-
-    def settle(c):
-        for e in range(2):
-            i = 2 * c + e
-            arrived(rs.at[i, 1 - core], fw_r.at[i])
-            held[pl.ds(i, 1)] = rs[pl.ds(i, 1)]
+    def forward(i):
+        @pl.when(i > 0)
+        def _():
+            arrived(rs.at[i, core], st_r.at[i])
+
+        forward_copy(i).start()
+
+    def settle(i):
+        arrived(rs.at[i, 1 - core], fw_r.at[i])
+        held[pl.ds(i, 1)] = rs[pl.ds(i, 1)]
 
     def collect(g):
         def block(j, carry):
@@ -421,60 +426,96 @@
         mrun[u] = jnp.full((1, UROWS), LOW, F32)
         zrun[u] = jnp.zeros((1, UROWS), F32)
 
-    def pair(u, c):
-        keys = kbuf[c]
-        parts = [nt(keys, qx[u, 256 * h : 256 * h + 256, :]) for h in range(2)]
-        for h in range(2):
-            s = parts[h]
-            lanes_h = slice(256 * h, 256 * h + 256)
-            old = mrun[u, :, lanes_h]
-            new = jnp.maximum(old, jnp.max(s, axis=0, keepdims=True))
-            p = jnp.exp2((s - new) * EXP_SCALE)
-            zrun[u, :, lanes_h] = zrun[u, :, lanes_h] * jnp.exp2((old - new) * EXP_SCALE) + jnp.sum(
-                p, axis=0, keepdims=True
-            )
-            mrun[u, :, lanes_h] = new
-            mchunk[c, u, :, lanes_h] = new
-            prob[c, pl.ds(8 * u, 8), :, lanes_h] = p.astype(BF16).reshape(8, BLK, 256)
+    def score(u, c, h, into):
+        into[...] = nt(kbuf[c], qx[u, 256 * h : 256 * h + 256, :])
+
+    def soften(u, c, h, held_scores):
+        s = held_scores[...]
+        lanes_h = slice(256 * h, 256 * h + 256)
+        old = mrun[u, :, lanes_h]
+        new = jnp.maximum(old, jnp.max(s, axis=0, keepdims=True))
+        p = jnp.exp2((s - new) * EXP_SCALE)
+        zrun[u, :, lanes_h] = zrun[u, :, lanes_h] * jnp.exp2((old - new) * EXP_SCALE) + jnp.sum(
+            p, axis=0, keepdims=True
+        )
+        mrun[u, :, lanes_h] = new
+        mchunk[c, u, :, lanes_h] = new
+        prob[c, pl.ds(8 * u, 8), :, lanes_h] = p.astype(BF16).reshape(8, BLK, 256)
 
     def group(g):
         collect(g)
 
         def step(u, carry):
-            pair(u, g)
+            score(u, g, 1, s_odd)
+            soften(u, g, 0, s_even)
+            score(jnp.minimum(u + 1, 3), g, 0, s_even)
+            soften(u, g, 1, s_odd)
             return carry
 
+        score(0, g, 0, s_even)
         lax.fori_loop(0, 4, step, 0)
 
-    def step(c, carry):
-        forward(c)
-
-        @pl.when(c > 0)
+    def flow(i, carry):
+        @pl.when(i < NCOL)
         def _():
-            settle(c - 1)
-
-        return carry
-
-    lax.fori_loop(0, 6, step, 0)
-    for u in range(4):
+            stage_copy(i - IN_FLIGHT).wait_send()
+            stage_send(i, 0)
+
+        @pl.when(i >= LAG)
+        def _():
+            forward(i - LAG)
+
+        @pl.when(i > LAG)
+        def _():
+            settle(i - LAG - 1)
+
+        return carry
+
+    def unit(u, carry):
         query_unit(u)
-    group(0)
-    step(6, 0)
-    group(1)
+        return carry
+
+    lax.fori_loop(IN_FLIGHT + 1, 14, flow, 0)
+    lax.fori_loop(0, 4, unit, 0)
+    def positions(i, carry):
+        l8 = lax.broadcasted_iota(I32, (8, 128), 1)
+        a, b = tbs[NCTX + 1, 2 * i] * BLK, tbs[NCTX + 1, 2 * i + 1] * BLK
+        kpos[pl.ds(i, 1)] = (jnp.where(l8 < BLK, a, b) + l8 % BLK).reshape(1, 8, 128)
+        return carry
+
+    lax.fori_loop(0, SPAN // 128, positions, 0)
     own_q = lax.broadcasted_iota(I32, (128, 128), 0) // 8 + BLK * blk_b + 16 * t_own
     own_q = own_q == lax.broadcasted_iota(I32, (128, 128), 1)
-    for s in range(NZ):
+
+    def prepare(s, carry):
         arrived(iq.at[s], iq_r.at[s])
         arrived(iw.at[s], iw_r.at[s])
         w = jnp.broadcast_to(iw[s].reshape(1, 8, 128), (16, 8, 128)).reshape(128, 128)
         w = jnp.sum(jnp.where(own_q, w, 0.0), axis=1, keepdims=True)
         wcol[s] = jnp.broadcast_to(w * IDX_SCALE, (128, 128))
-        iqt[:, 128 * s : 128 * (s + 1)] = iq[s].astype(F32).T.astype(BF16)
-
-    step(7, 0)
-    group(2)
-    settle(7)
-    group(3)
+        iqt[:, pl.ds(pl.multiple_of(128 * s, 128), 128)] = iq[s].astype(F32).T.astype(BF16)
+        return carry
+
+    lax.fori_loop(0, NZ, prepare, 0)
+
+    lax.fori_loop(14, 10 + LAG, flow, 0)
+    settle(9)
+
+    def arrive_and_score(g, carry):
+        @pl.when(g > 0)
+        def _():
+            settle(8 + 2 * g)
+            settle(9 + 2 * g)
+
+        @pl.when(g < 3)
+        def _():
+            forward(10 + 2 * g)
+            forward(11 + 2 * g)
+
+        group(g)
+        return carry
+
+    lax.fori_loop(0, 4, arrive_and_score, 0)
 
     for u in range(4):
         scale = 1.0 / (zrun[u] * HEADS)
@@ -519,22 +560,16 @@
         keys = ikc[pl.ds(kt * (TILE // BLK), TILE // BLK)].reshape(TILE, DI)
         return nt(iq[s], keys)
 
-    def logit_tile(kt):
+    def logit_tile(kt, carry):
         acc = jnp.zeros((128, TILE), F32)
         for s in range(NZ):
             w = jnp.concatenate([wcol[s]] * (TILE // 128), axis=1)
             acc = acc + w * jnp.maximum(dots_of(s, kt), 0.0)
-        return jnp.sum(acc.reshape(16, 8, TILE), axis=1)
-
-    logit_tiles = [logit_tile(0)]
-
-    def positions(i, carry):
-        l8 = lax.broadcasted_iota(I32, (8, 128), 1)
-        a, b = tbs[NCTX + 1, 2 * i] * BLK, tbs[NCTX + 1, 2 * i + 1] * BLK
-        kpos[pl.ds(i, 1)] = (jnp.where(l8 < BLK, a, b) + l8 % BLK).reshape(1, 8, 128)
-        return carry
-
-    lax.fori_loop(0, SPAN // 128, positions, 0)
+        lbuf[kt] = jnp.sum(acc.reshape(16, 8, TILE), axis=1)
+        return carry
+
+    lax.fori_loop(0, SPAN // TILE, logit_tile, 0)
+
     q_pos = q_base + 16 * t_own + lax.broadcasted_iota(I32, (16, 128), 0)
     visible = jnp.concatenate(
         [jnp.concatenate([kpos[i]] * 2, axis=0) <= q_pos for i in range(SPAN // 128)], axis=1
@@ -547,10 +582,28 @@
     mine = tq[pl.ds(2 * half + core, 1)].reshape(16, SPAN) + tsib[pl.ds(half, 1)].reshape(16, SPAN).astype(F32)
     other = tq[pl.ds(2 * far + core, 1)].reshape(16, SPAN) + tsib[pl.ds(far, 1)].reshape(16, SPAN).astype(F32)
     tfar[0] = other.astype(BF16)
-    far_copy = remote(tfar.at[0], tfar.at[1], tf_s.at[0], tf_r.at[0], me, (z + 4) % NZ)
+    far_copy = remote(tfar.at[0], tfar.at[1], tf_s.at[0], tf_r.at[0], me, wrap(z + 4, NZ))
     far_copy.start()
-    logit_tiles += [logit_tile(kt) for kt in range(1, SPAN // TILE)]
-    logits = jnp.concatenate(logit_tiles, axis=1)
+
+    for finish in pending:
+        finish()
+
+    def drain_sel(d, carry):
+        sel_copy(d).wait_send()
+        return carry
+
+    def drain_stage(i, carry):
+        stage_copy(i).wait_send()
+        return carry
+
+    def drain_forward(i, carry):
+        forward_copy(i).wait_send()
+        return carry
+
+    lax.fori_loop(1, NCTX, drain_sel, 0)
+    lax.fori_loop(NCOL - IN_FLIGHT, NCOL, drain_stage, 0)
+    lax.fori_loop(0, NCOL, drain_forward, 0)
+    logits = jnp.concatenate([lbuf[kt] for kt in range(SPAN // TILE)], axis=1)
     masked = jnp.where(visible, logits, FLOOR)
     shifted = masked - jnp.max(masked, axis=1, keepdims=True)
     log_norm = jnp.log(jnp.sum(jnp.exp(shifted), axis=1, keepdims=True))
@@ -569,9 +622,8 @@
     klm[...] = jnp.broadcast_to(
         jnp.sum(jnp.where(spot, divergence, 0.0), axis=0, keepdims=True), (8, 128)
     )
-    pending.append(
-        send(klm, klr, kl_s.at[0], kl_r.at[0], src_ctx, 4 * blk_b + t_own)
-    )
+    kl_send = send(klm, klr, kl_s.at[0], kl_r.at[0], src_ctx, 4 * blk_b + t_own)
+    kl_send.start()
 
     KB = TILE // BLK
 
@@ -579,22 +631,25 @@
         part = pl.ds(kt * KB, KB)
         return remote(gsend.at[part], grecv.at[part], gs_s.at[kt], gs_r.at[kt], sib, z)
 
+    def kz_send(kt, t):
+        to = 2 * blk_b + half
+        return send(
+            kz.at[t, kt], kr.at[to, kt], kz_s.at[4 * t + kt], kz_r.at[4 * to + kt], src_ctx, 4 * core + t
+        )
+
     def cores_sum(kt):
-        here = slice(kt * KB, (kt + 1) * KB)
-        arrived(grecv.at[pl.ds(kt * KB, KB)], gs_r.at[kt])
+        here = pl.ds(kt * KB, KB)
+        arrived(grecv.at[here], gs_r.at[kt])
         both = gkf[here, pl.ds(32 * core, 32), :] + grecv[here].astype(F32)
-        to = 2 * blk_b + half
         for t in range(4):
-            kz[t, kt] = both[:, 8 * t : 8 * t + 8, :].reshape(KB * 8, DI).astype(BF16)
-            pending.append(
-                send(
-                    kz.at[t, kt], kr.at[to, kt], kz_s.at[4 * t + kt], kz_r.at[4 * to + kt],
-                    src_ctx, 4 * core + t,
-                )
-            )
+            kz[t, pl.ds(kt, 1)] = both[:, 8 * t : 8 * t + 8, :].reshape(1, KB * 8, DI).astype(BF16)
+            kz_send(kt, t).start()
 
     for kt in range(SPAN // TILE):
-        g = gradient[:, kt * TILE : (kt + 1) * TILE]
+        gbuf[kt] = gradient[:, kt * TILE : (kt + 1) * TILE]
+
+    def backward(kt, carry):
+        g = gbuf[kt]
         g = jnp.broadcast_to(g.reshape(16, 1, TILE), (16, 8, TILE)).reshape(128, TILE)
         for s in range(NZ):
             dots = dots_of(s, kt)
@@ -602,42 +657,53 @@
             lanesum = weighted[:, 0:128]
             for i in range(1, TILE // 128):
                 lanesum = lanesum + weighted[:, 128 * i : 128 * (i + 1)]
-            gwacc[s] = lanesum if kt == 0 else gwacc[s] + lanesum
+            gwacc[s] = jnp.where(kt == 0, 0.0, gwacc[s]) + lanesum
             w = jnp.concatenate([wcol[s]] * (TILE // 128), axis=1)
             prob[kt, 2 * s : 2 * s + 2] = (
                 jnp.where(dots > 0.0, g * w, 0.0).astype(BF16).reshape(2, BLK, TILE)
             )
         part = jnp.dot(iqt[...], prob[kt, 0 : 2 * NZ].reshape(NZ * 128, TILE), preferred_element_type=F32)
-        here = slice(kt * KB, (kt + 1) * KB)
+        here = pl.ds(kt * KB, KB)
         gkf[here] = part.T.reshape(KB, BLK, DI)
         gsend[here] = gkf[here, pl.ds(32 * (1 - core), 32), :].astype(BF16)
         swap(kt).start()
-        if kt > 0:
+
+        @pl.when(kt > 0)
+        def _():
             cores_sum(kt - 1)
+
+        return carry
+
+    lax.fori_loop(0, SPAN // TILE, backward, 0)
+
     unspread = jnp.where(
         lax.broadcasted_iota(I32, (16, 128), 0) == lax.broadcasted_iota(I32, (16, 128), 1) // 8, 1.0, 0.0
     )
     diag_j = lax.broadcasted_iota(I32, (128, 128), 0) % 8 == lax.broadcasted_iota(I32, (128, 128), 1)
-    for s in range(NZ):
-        gq = jnp.dot(
-            jnp.concatenate(
-                [prob[kt, 2 * s : 2 * s + 2].reshape(128, TILE) for kt in range(SPAN // TILE)], axis=1
-            ),
-            ikc[...].reshape(SPAN, DI), preferred_element_type=F32
-        )
-        gqm[s, 0:128, :] = gq.astype(BF16)
+    def query_grad(s, carry):
+        factor = jnp.concatenate(
+            [prob[kt, pl.ds(2 * s, 2)].reshape(128, TILE) for kt in range(SPAN // TILE)], axis=1
+        )
+        gq = jnp.dot(factor, ikc[...].reshape(SPAN, DI), preferred_element_type=F32)
         gw = jnp.sum(gwacc[s], axis=1, keepdims=True) * IDX_SCALE
         gw = jnp.dot(
             unspread, jnp.where(diag_j, gw, 0.0), preferred_element_type=F32, precision=lax.Precision.HIGHEST
         )
-        gqm[s, 128:144, :] = gw.astype(BF16)
+        gqm[pl.ds(s, 1), 0:128, :] = gq.astype(BF16).reshape(1, 128, DI)
+        gqm[pl.ds(s, 1), 128:144, :] = gw.astype(BF16).reshape(1, 16, DI)
+        return carry
+
+    lax.fori_loop(0, NZ, query_grad, 0)
     cores_sum(SPAN // TILE - 1)
-    for s in range(NZ):
-        pending.append(
-            send(
-                gqm.at[s], gqr.at[4 * blk_b + t_own], gq_s.at[s], gq_r.at[4 * blk_b + t_own], src_ctx, s
-            )
-        )
+
+    def gq_send(s):
+        return send(gqm.at[s], gqr.at[4 * blk_b + t_own], gq_s.at[s], gq_r.at[4 * blk_b + t_own], src_ctx, s)
+
+    def gq_start(s, carry):
+        gq_send(s).start()
+        return carry
+
+    lax.fori_loop(0, NZ, gq_start, 0)
     for kt in range(SPAN // TILE):
         swap(kt).wait_send()
     for b in range(2):
@@ -660,7 +726,7 @@
         return jnp.concatenate(parts, axis=0).astype(BF16)
 
     def owner_of(i):
-        return (me + i) % NCTX
+        return wrap(me + i, NCTX)
 
     def owner_send(i, carry):
         o = owner_of(i)
@@ -679,8 +745,15 @@
     code = jnp.sum(wide, axis=0, keepdims=True) + (
         lax.broadcasted_iota(I32, (1, 1024), 1) % 8
     ).astype(F32)
-    row = lax.broadcasted_iota(I32, (512, 1024), 0).astype(F32)
-    hot = jnp.where(row == code, 1.0, 0.0).astype(BF16)
+    row = lax.broadcasted_iota(I32, (128, 1024), 0).astype(F32)
+
+    def sum_blocks(i, carry):
+        hot = jnp.where(row == code - (128 * i).astype(F32), 1.0, 0.0).astype(BF16)
+        gk_out[pl.ds(pl.multiple_of(128 * i, 128), 128), :] = jnp.dot(
+            hot, pr[...].reshape(1024, DI), preferred_element_type=F32
+        )
+        return carry
+
 
     arrived(klr, kl_r.at[0])
     kl_out[...] = klr[...]
@@ -695,28 +768,18 @@
         return carry
 
     lax.fori_loop(1, NCTX, owner_wait, 0)
-    gk_out[...] = jnp.dot(hot, pr[...].reshape(1024, DI), preferred_element_type=F32)
-
-    for finish in pending:
-        finish()
+    lax.fori_loop(0, 4, sum_blocks, 0)
+
+    kl_send.finish()
     far_copy.wait_send()
 
-    def drain_sel(d, carry):
-        sel_copy(d).wait_send()
-        return carry
-
-    def drain_stage(i, carry):
-        stage_copy(i).wait_send()
-        return carry
-
-    lax.fori_loop(1, NCTX, drain_sel, 0)
-    lax.fori_loop(1, NCOL, drain_stage, 0)
-
-    def drain_forward(i, carry):
-        forward_copy(i).wait_send()
-        return carry
-
-    lax.fori_loop(0, NCOL, drain_forward, 0)
+    def drain_gradients(s, carry):
+        gq_send(s).finish()
+        for t in range(2):
+            kz_send(s % 4, s // 4 * 2 + t).finish()
+        return carry
+
+    lax.fori_loop(0, NZ, drain_gradients, 0)
 
 
 def unpack(gk, gq, kl, gk_out, gq_out, gw_out, kl_out):
@@ -741,6 +804,7 @@
         V((NCOL, 11, BLK, 128), BF16), V((NCOL, 2, 11, BLK, 128), BF16),
         V((NCOL, 2, 11, BLK, 128), BF16), V((4, 512, EXT), BF16),
         V((4, 72, 32, 128), BF16), V((4, 72, 32, 128), BF16), V((4, UROWS, EXT), BF16),
+        V((512, 256), F32), V((512, 256), F32),
         V((4, 32, BLK, UROWS), BF16), V((4, 1, UROWS), F32), V((4, 1, UROWS), F32),
         V((4, 4, 1, UROWS), F32), V((4, 4, 16, UROWS), BF16),
         V((2, SEL, BLK, UROWS), BF16), V((2, SEL, BLK, 128), BF16),
@@ -753,6 +817,7 @@
         V((4, 4, SEL * 2, DI), BF16), V((4, 4, SEL * 2, DI), BF16), V((2, SEL + 1, 8, DI), F32),
         V((NCTX, 32, DI), BF16), V((NCTX, 32, DI), BF16),
         V((NZ, 144, DI), BF16), V((8, 144, DI), BF16), V((8, 128), F32), V((8, 128), F32),
+        V((4, 16, 512), F32), V((4, 16, 512), F32),
         dma((BLK // 2,)), dma((16,)), dma((1,)), dma((NCTX,)), dma((NCTX,)), dma((2,)),
         dma((4,)), dma((4,)), dma((8,)), dma((8,)), dma((8,)), dma((8,)),
         dma((NCOL,)), dma((NCOL,)), dma((NCOL,)), dma((NCOL,)),

time: 106 us -> 104 us (0.981)
  Pallas kernels: 106 us -> 103 us
    pallas_call x1, Pallas kernels: 104 us -> 101 us  [local(): pl.pallas_call(kernel, out_shape=[jax.ShapeDtypeStruct((BLK * 8, DI), F32...]
where the time goes in v3:
time: 104 us
  Pallas kernels  103 us (99%)
    pallas_call x1, Pallas kernels, local(): pl.pallas_call(kernel, out_shape=[jax.ShapeDtypeStruct((BLK * 8, DI), F32...  101 us

profile of v3, /device:TPU:1, one launch (start us, length us, event | category | flops | bytes accessed | tf_op | source)
XLA Modules:
  0.0 103.8 jit_solution(2330115902312940311)
XLA Ops:
  0.6 101.2 %indexer_step.1 = (f32[512,128]{1,0:T(8,128)}, bf16[8,144,128]{2,1,0:T(8,128)(2,1)}, f32[8,128]{1,0:T(8,128)}) custom-call(s32[2,32]{1,0:T(2,128)} %sel_in.1, bf16[9,64,4096]{2,1,0:T(8,128)(2,1)} %bitcast.10, bf16[64,64,128]{2,1,0:T(8,128)(2,1)} %bitcast.12, bf16[16,9,64,128]{3,2,1,0:T(8,128)(2,1)} %bitcast.11, bf16[1024,128]{1,0:T(8,128)(2,1)} %bitcast.13, ...), custom_call_target="tpu_custom_call" | custom-call | tf_op jit(solution)/shard_map/indexer_step/pallas_call | solution.py:827
  101.9 2.0 %unpack.1 = (f32[64,8,128]{2,1,0:T(8,128)}, f32[128,8,128]{2,1,0:T(8,128)}, f32[8,128]{1,0:T(8,128)}, f32[16]{0:T(128)}) custom-call(f32[512,128]{1,0:T(8,128)} %get-tuple-element.11.gk, bf16[8,144,128]{2,1,0:T(8,128)(2,1)} %get-tuple-element.12.gq, f32[8,128]{1,0:T(8,128)} %get-tuple-element.13.kl), custom_call_target="tpu_custom_call" | custom-call | tf_op jit(solution)/shard_map/unpack/pallas_call | solution.py:849

commit v4 on v3

--- a/solution.py
+++ b/solution.py
@@ -128,6 +128,25 @@
 
     pending = []
 
+    barrier = pltpu.get_barrier_semaphore()
+
+    def greet_plane(d, carry):
+        pl.semaphore_signal(
+            barrier, inc=1, device_id={"ctx": wrap(me + d, NCTX), "head": z}, device_id_type=MESH
+        )
+        return carry
+
+    def greet_column(d, carry):
+        for c in range(2):
+            pl.semaphore_signal(
+                barrier, inc=1, device_id={"ctx": 2 * k + c, "head": wrap(z + d, NZ)}, device_id_type=MESH
+            )
+        return carry
+
+    lax.fori_loop(1, NCTX, greet_plane, 0)
+    lax.fori_loop(1, NZ, greet_column, 0)
+    selall[pl.ds(me, 1), 0:2, 0:SEL] = sel_in[...].reshape(1, 2, SEL)
+
     def load_query(h):
         return pltpu.make_async_copy(
             mq_hbm.at[h],
@@ -150,24 +169,6 @@
 
     lax.fori_loop(0, BLK // 2, start_latents, 0)
     load_ik.start()
-    barrier = pltpu.get_barrier_semaphore()
-
-    def greet_plane(d, carry):
-        pl.semaphore_signal(
-            barrier, inc=1, device_id={"ctx": wrap(me + d, NCTX), "head": z}, device_id_type=MESH
-        )
-        return carry
-
-    def greet_column(d, carry):
-        for c in range(2):
-            pl.semaphore_signal(
-                barrier, inc=1, device_id={"ctx": 2 * k + c, "head": wrap(z + d, NZ)}, device_id_type=MESH
-            )
-        return carry
-
-    lax.fori_loop(1, NCTX, greet_plane, 0)
-    lax.fori_loop(1, NZ, greet_column, 0)
-    selall[pl.ds(me, 1), 0:2, 0:SEL] = sel_in[...].reshape(1, 2, SEL)
     iwf[...] = iw_in[...].astype(F32)
 
     def turn_query(h, carry):

time: 104 us -> 103 us (level)
  no operation moved by 1% of the time
where the time goes in v4:
time: 103 us
  Pallas kernels  102 us (99%)
    pallas_call x1, Pallas kernels, local(): pl.pallas_call(kernel, out_shape=[jax.ShapeDtypeStruct((BLK * 8, DI), F32...  101 us

profile of v4, /device:TPU:1, one launch (start us, length us, event | category | flops | bytes accessed | tf_op | source)
XLA Modules:
  0.0 103.1 jit_solution(3177879289132138497)
XLA Ops:
  0.6 100.5 %indexer_step.1 = (f32[512,128]{1,0:T(8,128)}, bf16[8,144,128]{2,1,0:T(8,128)(2,1)}, f32[8,128]{1,0:T(8,128)}) custom-call(s32[2,32]{1,0:T(2,128)} %sel_in.1, bf16[9,64,4096]{2,1,0:T(8,128)(2,1)} %bitcast.10, bf16[64,64,128]{2,1,0:T(8,128)(2,1)} %bitcast.12, bf16[16,9,64,128]{3,2,1,0:T(8,128)(2,1)} %bitcast.11, bf16[1024,128]{1,0:T(8,128)(2,1)} %bitcast.13, ...), custom_call_target="tpu_custom_call" | custom-call | tf_op jit(solution)/shard_map/indexer_step/pallas_call | solution.py:828
  101.2 2.0 %unpack.1 = (f32[64,8,128]{2,1,0:T(8,128)}, f32[128,8,128]{2,1,0:T(8,128)}, f32[8,128]{1,0:T(8,128)}, f32[16]{0:T(128)}) custom-call(f32[512,128]{1,0:T(8,128)} %get-tuple-element.11.gk, bf16[8,144,128]{2,1,0:T(8,128)(2,1)} %get-tuple-element.12.gq, f32[8,128]{1,0:T(8,128)} %get-tuple-element.13.kl), custom_call_target="tpu_custom_call" | custom-call | tf_op jit(solution)/shard_map/unpack/pallas_call | solution.py:850
